TPU v7x, 512 devices: a whole 4x8x8 slice. The times are simulated.
512 devices in a mesh: heads: 8 (over z), seq: 64 (over y, x, core).
Axes of the slice: x: 4, y: 8, z: 8, core: 2. Of those that a mesh axis runs over, the one named last changes fastest.
Arguments:
- tokens: bfloat16 [16, 16384], P(None, 'seq')
- norm_gain: bfloat16 [16384], P('seq'), may hold values from 0.099609375 to 1.8984375
- w_query: bfloat16 [16384, 16384], P('seq', 'heads'), may hold values from -0.046875 to 0.046875
- w_kv: bfloat16 [16384, 2048], P('seq', 'heads'), may hold values from -0.046875 to 0.046875
- w_out: bfloat16 [16384, 16384], P('heads', 'seq'), may hold values from -0.125 to 0.125
- key_cache: bfloat16 [8, 16, 16384, 128], P('heads', None, 'seq')
- value_cache: bfloat16 [8, 16, 16384, 128], P('heads', None, 'seq'), may hold values from -6 to 6
- lengths: int32 [16], replicated, may hold values from 1 to 16384, as said below
- positions: int32 [16], replicated, may hold values from 0 to 8191
Outputs:
- outputs: float32 [2, 16, 16384], P(None, None, 'seq')
Inputs may be any that keep to these rules, and one draw needn't show every extreme that they name: `lengths`: some row has all 16384 cached positions valid in every draw.
All inputs are finite; a program needn't handle non-finite values.
Results may differ from a plain program's by a relative error of at most 0.028.
Values sent between devices are 32-bit elements; how exact they have to be, the bound alone decides.
No kernel may reach another device: no remote copies, remote signals or barrier semaphores. Data moves between devices by JAX's collectives and lax.ppermute only.
A program may use at most 64 MiB of HBM per device.

v0:
```python
import math

import jax
import jax.numpy as jnp
from jax import lax
from jax.sharding import PartitionSpec as P

D = 16384
STEPS = 2


EPSILON = 1e-05
ROPE_BASE = 500000.0
FILLER = -1e30


def rotary(vectors, places):
    half_width = vectors.shape[-1] // 2
    freqs = ROPE_BASE ** (-(jnp.arange(half_width, dtype=jnp.float32) * 2.0 / vectors.shape[-1]))
    angles = places.astype(jnp.float32)[:, None] * freqs[None, :]
    angles = angles.reshape(angles.shape[:1] + (1,) * (vectors.ndim - 2) + angles.shape[1:])
    cosine = jnp.cos(angles)
    sine = jnp.sin(angles)
    first = vectors[..., :half_width]
    second = vectors[..., half_width:]
    return jnp.concatenate(
        [first * cosine - second * sine, second * cosine + first * sine], axis=-1
    )


def per_device(tokens, norm_gain, w_query, w_kv, w_out, key_cache, value_cache, lengths, positions):
    rows_here = tokens.shape[0]
    seq_here = key_cache.shape[2]
    head_dim = key_cache.shape[3]
    group_heads = w_query.shape[1] // head_dim
    scale = 1.0 / math.sqrt(head_dim)
    keys_local = key_cache[0]
    values_local = value_cache[0]
    offset = lax.axis_index("seq") * seq_here
    visible = (offset + jnp.arange(seq_here, dtype=jnp.int32))[None, :] < lengths[:, None]
    visible = visible[:, None, :]
    gain_wide = norm_gain.astype(jnp.float32)
    state = tokens
    own_keys = []
    own_values = []
    results = []
    for decode_step in range(STEPS):
        wide = state.astype(jnp.float32)
        gained = (wide * gain_wide[None, :]).astype(jnp.bfloat16)
        squares, query_raw, kv_raw = lax.psum(
            (
                jnp.sum(wide * wide, axis=1),
                jnp.dot(gained, w_query, preferred_element_type=jnp.float32),
                jnp.dot(gained, w_kv, preferred_element_type=jnp.float32),
            ),
            "seq",
        )
        inverse = lax.rsqrt(squares / D + EPSILON)
        places = positions + decode_step
        queries = rotary(
            (query_raw * inverse[:, None]).reshape(rows_here, group_heads, head_dim), places
        ).astype(jnp.bfloat16)
        kv_scaled = (kv_raw * inverse[:, None]).reshape(rows_here, 2, head_dim)
        own_keys.append(rotary(kv_scaled[:, 0], places).astype(jnp.bfloat16))
        own_values.append(kv_scaled[:, 1].astype(jnp.bfloat16))
        fresh_keys = jnp.stack(own_keys, 1)
        fresh_values = jnp.stack(own_values, 1)
        scores = (
            jnp.einsum("bjd,btd->bjt", queries, keys_local, preferred_element_type=jnp.float32)
            * scale
        )
        new_scores = (
            jnp.einsum("bjd,bnd->bjn", queries, fresh_keys, preferred_element_type=jnp.float32)
            * scale
        )
        local_top = jnp.max(jnp.where(visible, scores, FILLER), axis=-1)
        whole_top = jnp.maximum(lax.pmax(local_top, "seq"), jnp.max(new_scores, axis=-1))
        probs = jnp.where(visible, jnp.exp(scores - whole_top[..., None]), 0.0)
        weighted = jnp.einsum(
            "bjt,btd->bjd",
            probs.astype(jnp.bfloat16),
            values_local,
            preferred_element_type=jnp.float32,
        )
        total, weighted = lax.psum((jnp.sum(probs, axis=-1), weighted), "seq")
        new_probs = jnp.exp(new_scores - whole_top[..., None])
        total = total + jnp.sum(new_probs, axis=-1)
        weighted = weighted + jnp.einsum(
            "bjn,bnd->bjd",
            new_probs.astype(jnp.bfloat16),
            fresh_values,
            preferred_element_type=jnp.float32,
        )
        attended = (
            (weighted / total[..., None])
            .astype(jnp.bfloat16)
            .reshape(rows_here, group_heads * head_dim)
        )
        partial_out = jnp.dot(attended, w_out, preferred_element_type=jnp.float32)
        output = lax.psum(partial_out, "heads")
        results.append(output)
        state = (wide + output).astype(jnp.bfloat16)
    return jnp.stack(results, 0)


def solution(mesh):
    in_specs = (
        P(None, "seq"),
        P("seq"),
        P("seq", "heads"),
        P("seq", "heads"),
        P("heads", "seq"),
        P("heads", None, "seq", None),
        P("heads", None, "seq", None),
        P(),
        P(),
    )
    out_specs = P(None, None, "seq")
    return jax.shard_map(
        per_device, mesh=mesh, in_specs=in_specs, out_specs=out_specs, check_vma=False
    )
```

profile of v0, /device:TPU:1, one launch (start us, length us, event | category | flops | bytes accessed | tf_op | source)
XLA Modules:
  0.0 1631.7 jit_solution(7808185464421248969)
XLA Ops:
  6.5 0.7 convert_element_type.69
  7.3 2.2 fusion.48
  9.5 0.0 all-reduce.9.cloned.1.call-start
  9.5 0.1 fusion.28
  9.7 0.7 copy-done.4
  10.4 0.1 fusion.46
  10.5 247.4 %all-reduce.1 = (f32[16]{0:T(128)S(1)}, f32[16,256]{1,0:T(8,128)S(1)}) all-reduce(f32[16]{0:T(128)S(1)} %fusion.28, f32[16,256]{1,0:T(8,128)S(1)} %fusion.46), channel_id=1, replica_groups=mesh['heads'=8,'seq'=64] {'seq'}, use_global_device_ids=true, to_apply=%region_2.0 | all-reduce | flops 4112 | bytes 32896 | tf_op jit(solution)/shard_map/psum | solution.py:50
  257.9 0.1 broadcast_multiply_fusion.1
  258.0 0.6 copy-done.6
  258.7 0.6 copy-done.8
  259.3 0.1 slice-done
  259.3 0.1 subtract_convert_fusion.3
  259.5 0.6 copy-done.7
  260.1 0.1 broadcast_compare_fusion
  260.2 0.1 maximum_bitcast_fusion
  260.3 1.0 multiply_bitcast_fusion.1
  261.3 0.1 subtract_convert_fusion.1
  261.4 0.2 fusion.30
  261.7 0.5 select_reduce_fusion.1
  262.2 131.0 %pmax.14 = f32[16,16]{1,0:T(8,128)S(1)} all-reduce(f32[16,16]{1,0:T(8,128)S(1)} %get-tuple-element.29), channel_id=1, replica_groups=mesh['heads'=8,'seq'=64] {'seq'}, use_global_device_ids=true, to_apply=%region_4.5 | all-reduce | flops 256 | bytes 2048 | tf_op jit(solution)/shard_map/pmax | solution.py:77
  393.2 0.2 fusion.8
  393.4 1.0 fusion.4
  394.4 126.2 %psum.88 = f32[16,16]{1,0:T(8,128)S(1)} all-reduce(f32[16,16]{1,0:T(8,128)S(1)} %fusion.8), channel_id=1, replica_groups=mesh['heads'=8,'seq'=64] {'seq'}, use_global_device_ids=true, to_apply=%region_8.9 | all-reduce | flops 256 | bytes 2048 | tf_op jit(solution)/shard_map/psum | solution.py:85
  520.7 0.0 all-reduce.11.cloned.1.call-start
  520.7 183.5 %all-reduce.9.cloned.1.call-done = f32[16,16,128]{2,1,0:T(8,128)} async-done(((f32[16,16,128]{2,1,0:T(8,128)}), f32[16,16,128]{2,1,0:T(8,128)}) %all-reduce.9.cloned.1.call-update) | async-done | bytes 131088 | tf_op jit(solution)/shard_map/psum | solution.py:85
  704.2 1.0 divide_convert_fusion
  705.3 1.5 fusion.22
  706.7 23.7 %psum.89 = f32[16,256]{1,0:T(8,128)S(1)} all-reduce(f32[16,256]{1,0:T(8,128)S(1)} %fusion.22), channel_id=1, replica_groups=mesh['heads'=8,'seq'=64] {'heads'}, use_global_device_ids=true, to_apply=%region_9.10 | all-reduce | flops 4096 | bytes 32768 | tf_op jit(solution)/shard_map/psum | solution.py:100
  730.5 0.1 fusion.26
  730.6 0.1 fusion.50
  730.7 0.9 fusion.52
  731.6 246.8 %all-reduce = (f32[16]{0:T(128)S(1)}, f32[16,256]{1,0:T(8,128)S(1)}) all-reduce(f32[16]{0:T(128)S(1)} %get-tuple-element.9, f32[16,256]{1,0:T(8,128)S(1)} %fusion.50), channel_id=1, replica_groups=mesh['heads'=8,'seq'=64] {'seq'}, use_global_device_ids=true, to_apply=%region_12.13 | all-reduce | flops 4112 | bytes 32896 | tf_op jit(solution)/shard_map/psum | solution.py:50
  978.5 0.1 broadcast_multiply_fusion
  978.7 0.1 fusion.54
  978.8 182.8 %all-reduce.11.cloned.1.call-done = f32[16,2048]{1,0:T(8,128)} async-done(((f32[16,2048]{1,0:T(8,128)}), f32[16,2048]{1,0:T(8,128)}) %all-reduce.11.cloned.1.call-update) | async-done | bytes 131088 | tf_op jit(solution)/shard_map/psum | solution.py:50
  1161.6 1.0 multiply_bitcast_fusion
  1162.6 0.1 subtract_convert_fusion
  1162.7 0.5 select_reduce_fusion
  1163.2 124.6 %pmax.15 = f32[16,16]{1,0:T(8,128)S(1)} all-reduce(f32[16,16]{1,0:T(8,128)S(1)} %get-tuple-element.31), channel_id=1, replica_groups=mesh['heads'=8,'seq'=64] {'seq'}, use_global_device_ids=true, to_apply=%region_14.15 | all-reduce | flops 256 | bytes 2048 | tf_op jit(solution)/shard_map/pmax | solution.py:77
  1287.9 0.2 fusion.67
  1288.1 0.2 fusion.10
  1288.3 1.0 fusion.2
  1289.3 128.4 %psum.94 = f32[16,16]{1,0:T(8,128)S(1)} all-reduce(f32[16,16]{1,0:T(8,128)S(1)} %fusion.10), channel_id=1, replica_groups=mesh['heads'=8,'seq'=64] {'seq'}, use_global_device_ids=true, to_apply=%region_19.20 | all-reduce | flops 256 | bytes 2048 | tf_op jit(solution)/shard_map/psum | solution.py:85
  1417.8 181.7 %all-reduce.13.cloned.1.call-done = f32[16,16,128]{2,1,0:T(8,128)} async-done(((f32[16,16,128]{2,1,0:T(8,128)}), f32[16,16,128]{2,1,0:T(8,128)}) %all-reduce.13.cloned.1.call-update) | async-done | bytes 131088 | tf_op jit(solution)/shard_map/psum | solution.py:85
  1599.4 1.1 fusion.1
  1600.6 0.2 convolution_bitcast_fusion
  1600.8 23.7 %psum.95 = f32[1,16,256]{2,1,0:T(8,128)S(1)} all-reduce(f32[1,16,256]{2,1,0:T(8,128)S(1)} %convolution_bitcast_fusion), channel_id=1, replica_groups=mesh['heads'=8,'seq'=64] {'heads'}, use_global_device_ids=true, to_apply=%region_21.22 | all-reduce | flops 4096 | bytes 32768 | tf_op jit(solution)/shard_map/psum | solution.py:100
  1624.5 0.6 pad_maximum_fusion.2
  (43 shorter events, 0.4 us)
Async XLA Ops:
  6.5 255.1 %copy-start = (bf16[1,16,256,128]{3,2,1,0:T(8,128)(2,1)S(1)}, bf16[1,16,256,128]{3,2,1,0:T(8,128)(2,1)}, u32[]{:S(2)}) copy-start(bf16[1,16,256,128]{3,2,1,0:T(8,128)(2,1)} %param.14) | copy-start | bytes 3145732
  6.5 253.7 %all-reduce.7.cloned.1.call-start = ((), (), s32[]{:S(2)}) async-start(), calls=%async_computation | async-start | bytes 262144 | tf_op jit(solution)/shard_map/psum | solution.py:50
  7.3 2.3 copy-start.5
  9.4 0.9 copy-start.4
  9.5 694.8 %all-reduce.9.cloned.1.call-start = ((), (), s32[]{:S(2)}) async-start(), calls=%async_computation.1 | async-start | bytes 262144 | tf_op jit(solution)/shard_map/psum | solution.py:85
  258.0 0.6 copy-start.6
  258.6 0.7 copy-start.8
  258.6 0.7 slice-start
  259.5 0.7 copy-start.7
  261.4 132.0 %copy-start.2 = (bf16[1,16,256,128]{3,2,1,0:T(8,128)(2,1)S(1)}, bf16[1,16,256,128]{3,2,1,0:T(8,128)(2,1)}, u32[]{:S(2)}) copy-start(bf16[1,16,256,128]{3,2,1,0:T(8,128)(2,1)} %param.15) | copy-start | bytes 3145732
  394.4 336.3 %copy-start.1 = (bf16[256,2048]{1,0:T(8,128)(2,1)S(1)}, bf16[256,2048]{1,0:T(8,128)(2,1)}, u32[]{:S(2)}) copy-start(bf16[256,2048]{1,0:T(8,128)(2,1)} %param.11) | copy-start | bytes 3145732
  520.7 640.9 %all-reduce.11.cloned.1.call-start = ((), (), s32[]{:S(2)}) async-start(), calls=%async_computation.2 | async-start | bytes 262144 | tf_op jit(solution)/shard_map/psum | solution.py:50
  978.6 620.8 %all-reduce.13.cloned.1.call-start = ((), (), s32[]{:S(2)}) async-start(), calls=%async_computation.3 | async-start | bytes 262144 | tf_op jit(solution)/shard_map/psum | solution.py:85
  1288.3 312.2 %copy-start.3 = (bf16[2048,256]{1,0:T(8,128)(2,1)S(1)}, bf16[2048,256]{1,0:T(8,128)(2,1)}, u32[]{:S(2)}) copy-start(bf16[2048,256]{1,0:T(8,128)(2,1)} %param.13) | copy-start | bytes 3145732
Sparse Core Ops, SparseCore 0:
  10.8 190.1 all-reduce.6
  520.8 183.3 all-reduce.8
  978.7 182.8 all-reduce.10
  1417.8 181.5 all-reduce.12
where the time goes:
time: 1640 us; the launch traced here: 1630 us
  blocking collectives  1050 us (64%)
  waiting for transfers between devices  548 us (33%)
    psum x2, blocking collectives, per_device(): lax.psum((jnp.sum(wide * wide, axis=1), jnp.dot(gained, w_query, preferre...  494 us
    psum x2, waiting for transfers between devices, per_device(): total, weighted = lax.psum((jnp.sum(probs, axis=-1), weighted), 'seq')  365 us
    pmax x2, blocking collectives, per_device(): lax.pmax(local_top, 'seq')  256 us
    psum x2, blocking collectives, per_device(): total, weighted = lax.psum((jnp.sum(probs, axis=-1), weighted), 'seq')  255 us
    psum x2, waiting for transfers between devices, per_device(): lax.psum((jnp.sum(wide * wide, axis=1), jnp.dot(gained, w_query, preferre...  183 us
    psum x2, blocking collectives, per_device(): output = lax.psum(partial_out, 'heads')  47.4 us
  transfers between devices with their start and end apart: 4, of which 3 were waited for; matrix products, arithmetic and copies ran while one was open for 0% of the time, Pallas kernels for 0%

commit v1 on v0

v1 whole, which is shorter than its diff:
```python
import math

import jax
import jax.numpy as jnp
from jax import lax
from jax.sharding import Mesh, PartitionSpec as P

D = 16384
STEPS = 2
EPSILON = 1e-05
ROPE_BASE = 500000.0
FILLER = -3e38
CHIPS_Y = 8
INNER = ("x", "core")
SEQ = ("y", "x", "core")


def scatter(pieces, axes):
    return lax.all_to_all(pieces, axes, 0, 0, tiled=True)


def gather(piece, axes, size):
    copies = jnp.broadcast_to(piece[None], (size,) + piece.shape)
    return lax.all_to_all(copies, axes, 0, 0, tiled=True)


def angles_of(places, head_dim):
    half = head_dim // 2
    freqs = ROPE_BASE ** (-(jnp.arange(half, dtype=jnp.float32) * 2.0 / head_dim))
    angles = places.astype(jnp.float32)[:, None] * freqs[None, :]
    return jnp.cos(angles)[:, None], jnp.sin(angles)[:, None]


def rotary(vectors, cosine, sine):
    half = vectors.shape[-1] // 2
    first = vectors[..., :half]
    second = vectors[..., half:]
    return jnp.concatenate(
        [first * cosine - second * sine, second * cosine + first * sine], axis=-1
    )


def per_device(sizes, tokens, norm_gain, w_query, w_kv, w_out, key_cache, value_cache, lengths, positions):
    heads_size, y_size, inner_size = sizes
    rows = tokens.shape[0]
    seq_here = key_cache.shape[2]
    head_dim = key_cache.shape[3]
    group_heads = w_query.shape[1] // head_dim
    rows_own = rows // inner_size
    scale = 1.0 / math.sqrt(head_dim)
    keys_local = key_cache[0]
    values_local = value_cache[0]
    offset = lax.axis_index(SEQ) * seq_here
    visible = (offset + jnp.arange(seq_here, dtype=jnp.int32))[None, :] < lengths[:, None]
    visible = visible[:, None, :]
    inner = lax.axis_index(INNER)
    own_positions = lax.dynamic_slice(positions, (inner * rows_own,), (rows_own,))
    gain_wide = norm_gain.astype(jnp.float32)
    state = tokens
    own_keys = []
    own_values = []
    results = []
    for decode_step in range(STEPS):
        wide = state.astype(jnp.float32)
        gained = (wide * gain_wide[None, :]).astype(jnp.bfloat16)
        squares = jnp.broadcast_to(jnp.sum(wide * wide, axis=1)[:, None], (rows, head_dim))
        projected = jnp.concatenate(
            [
                jnp.dot(gained, w_query, preferred_element_type=jnp.float32),
                jnp.dot(gained, w_kv, preferred_element_type=jnp.float32),
                squares,
            ],
            axis=1,
        )
        width = projected.shape[1]
        part = scatter(projected.reshape(inner_size, rows_own, width), INNER)
        part = gather(jnp.sum(part, axis=0), ("y",), y_size)
        part = jnp.sum(part, axis=0)
        inverse = lax.rsqrt(part[:, width - head_dim :] / D + EPSILON)
        cosine, sine = angles_of(own_positions + decode_step, head_dim)
        raw = part[:, : width - head_dim].reshape(rows_own, group_heads + 2, head_dim)
        vectors = raw * inverse[:, None]
        turned = rotary(vectors[:, : group_heads + 1], cosine, sine)
        own_keys.append(turned[:, group_heads].astype(jnp.bfloat16))
        own_values.append(vectors[:, group_heads + 1].astype(jnp.bfloat16))
        queries_own = turned[:, :group_heads]
        sent = jnp.concatenate([rotary(raw[:, :group_heads], cosine, sine), inverse[:, None]], axis=1)
        sent = gather(sent, INNER, inner_size).reshape(rows, group_heads + 1, head_dim)
        queries = (sent[:, :group_heads] * sent[:, group_heads:]).astype(jnp.bfloat16)
        scores = (
            jnp.einsum("bjd,btd->bjt", queries, keys_local, preferred_element_type=jnp.float32)
            * scale
        )
        top = jnp.max(jnp.where(visible, scores, FILLER), axis=-1)
        probs = jnp.where(visible, jnp.exp(scores - top[..., None]), 0.0)
        total = jnp.sum(probs, axis=-1)
        weighted = jnp.einsum(
            "bjt,btd->bjd",
            probs.astype(jnp.bfloat16),
            values_local,
            preferred_element_type=jnp.float32,
        )

        def send(top, total, weighted, axes, count):
            lead = weighted.shape[:-3] if axes == INNER else ()
            stats = jnp.stack([top, total], axis=1)
            stats = jnp.pad(stats, ((0, 0), (0, 0), (0, head_dim - group_heads)))
            block = jnp.concatenate([weighted, stats], axis=1)
            if axes == INNER:
                got = scatter(block.reshape(inner_size, rows_own, group_heads + 2, head_dim), axes)
            else:
                got = gather(block, axes, count)
            tops = got[:, :, group_heads, :group_heads]
            totals = got[:, :, group_heads + 1, :group_heads]
            top = jnp.max(tops, axis=0)
            factor = jnp.exp(tops - top[None])
            total = jnp.sum(factor * totals, axis=0)
            weighted = jnp.sum(factor[..., None] * got[:, :, :group_heads], axis=0)
            return top, total, weighted

        top, total, weighted = send(top, total, weighted, INNER, inner_size)
        top, total, weighted = send(top, total, weighted, ("y",), y_size)
        own_queries = queries_own.astype(jnp.bfloat16)
        fresh_keys = jnp.stack(own_keys, 1)
        fresh_values = jnp.stack(own_values, 1)
        new_scores = (
            jnp.einsum("bjd,bnd->bjn", own_queries, fresh_keys, preferred_element_type=jnp.float32)
            * scale
        )
        whole_top = jnp.maximum(top, jnp.max(new_scores, axis=-1))
        factor = jnp.exp(top - whole_top)
        new_probs = jnp.exp(new_scores - whole_top[..., None])
        total = total * factor + jnp.sum(new_probs, axis=-1)
        weighted = weighted * factor[..., None] + jnp.einsum(
            "bjn,bnd->bjd",
            new_probs.astype(jnp.bfloat16),
            fresh_values,
            preferred_element_type=jnp.float32,
        )
        stats = jnp.pad(total, ((0, 0), (0, head_dim - group_heads)))
        sent = jnp.concatenate([weighted, stats[:, None]], axis=1)
        sent = gather(sent, INNER, inner_size).reshape(rows, group_heads + 1, head_dim)
        attended = sent[:, :group_heads] / sent[:, group_heads, :group_heads][..., None]
        attended = attended.reshape(rows, group_heads * head_dim).astype(jnp.bfloat16)
        partial_out = jnp.dot(attended, w_out, preferred_element_type=jnp.float32)
        output = jnp.sum(gather(partial_out, ("heads",), heads_size), axis=0)
        results.append(output)
        state = (wide + output).astype(jnp.bfloat16)
    return jnp.stack(results, 0)


def solution(mesh):
    heads_size = mesh.shape["heads"]
    seq_size = mesh.shape["seq"]
    inner_size = seq_size // CHIPS_Y
    devices = mesh.devices.reshape(heads_size, CHIPS_Y, inner_size // 2, 2)
    fine = Mesh(devices, ("heads", "y", "x", "core"))
    in_specs = (
        P(None, SEQ),
        P(SEQ),
        P(SEQ, "heads"),
        P(SEQ, "heads"),
        P("heads", SEQ),
        P("heads", None, SEQ, None),
        P("heads", None, SEQ, None),
        P(),
        P(),
    )

    def body(*args):
        return per_device((heads_size, CHIPS_Y, inner_size), *args)

    return jax.shard_map(
        body, mesh=fine, in_specs=in_specs, out_specs=P(None, None, SEQ), check_vma=False
    )
```

time: 1640 us -> 178 us (0.11)
  blocking collectives: 1050 us -> 68.1 us
  waiting for transfers between devices: 548 us -> 48.4 us
  starting transfers between devices: 0.13 us -> 40.1 us
    psum x6 -> x0, blocking collectives: 796 us -> none  [the longest x2 494 us: per_device(): lax.psum((jnp.sum(wide * wide, axis=1), jnp.dot(gained, w_query, preferre...]
    psum x4 -> x0, waiting for transfers between devices: 548 us -> none  [the longest x2 365 us: per_device(): total, weighted = lax.psum((jnp.sum(probs, axis=-1), weighted), 'seq')]
    pmax x2 -> x0, blocking collectives: 256 us -> none  [per_device(): lax.pmax(local_top, 'seq')]
    all_to_all x0 -> x6, blocking collectives: none -> 68.1 us  [the longest x5 57.8 us: gather(): return lax.all_to_all(copies, axes, 0, 0, tiled=True)]
    all_to_all x0 -> x8, waiting for transfers between devices: none -> 48.4 us  [the longest x5 33.7 us: gather(): return lax.all_to_all(copies, axes, 0, 0, tiled=True)]
    all_to_all x0 -> x8, starting transfers between devices: none -> 40.1 us  [the longest x5 21.7 us: gather(): return lax.all_to_all(copies, axes, 0, 0, tiled=True)]
  transfers between devices with their start and end apart: 4 -> 8, of which waited for: 3 -> 8; matrix products, arithmetic and copies ran while one was open for 0% -> 1% of each run, Pallas kernels for 0% -> 0%
where the time goes in v1:
time: 178 us; the launch traced here: 177 us
  blocking collectives  68.1 us (38%)
  waiting for transfers between devices  48.4 us (27%)
  starting transfers between devices  40.1 us (23%)
  local copies, waits for them, and re-layouts  9.25 us (5%)
  matrix products  5.47 us (3%)
  other arithmetic  4.89 us (3%)
    all_to_all x5, blocking collectives, gather(): return lax.all_to_all(copies, axes, 0, 0, tiled=True)  57.8 us
    all_to_all x5, waiting for transfers between devices, gather(): return lax.all_to_all(copies, axes, 0, 0, tiled=True)  33.7 us
    all_to_all x5, starting transfers between devices, gather(): return lax.all_to_all(copies, axes, 0, 0, tiled=True)  21.7 us
    all_to_all x3, starting transfers between devices, scatter(): return lax.all_to_all(pieces, axes, 0, 0, tiled=True)  18.5 us
    all_to_all x3, waiting for transfers between devices, scatter(): return lax.all_to_all(pieces, axes, 0, 0, tiled=True)  14.7 us
    all_to_all x1, blocking collectives, scatter(): return lax.all_to_all(pieces, axes, 0, 0, tiled=True)  10.3 us
    broadcast_in_dim x10, local copies, waits for them, and re-layouts, gather(): copies = jnp.broadcast_to(piece[None], (size,) + piece.shape)  3.6 us
  transfers between devices with their start and end apart: 8, of which 8 were waited for; matrix products, arithmetic and copies ran while one was open for 1% of the time, Pallas kernels for 0%

profile of v1, /device:TPU:1, one launch (start us, length us, event | category | flops | bytes accessed | tf_op | source)
XLA Modules:
  0.0 176.7 jit_solution(9284225565445719371)
XLA Ops:
  0.0 0.9 fusion.39
  1.0 1.0 fusion.56
  2.0 1.5 fusion.58
  3.6 0.7 reshape.239
  4.3 10.2 %all-to-all-start = ((f32[8,2,2432]{2,1,0:T(2,128)}), f32[8,2,2432]{2,1,0:T(2,128)S(1)}, u32[]{:S(2)}, u32[]{:S(2)}) async-start(f32[8,2,2432]{2,1,0:T(2,128)} %reshape.239), calls=%async_computation | async-start | bytes 311296 | tf_op jit(solution)/shard_map/all_to_all | solution.py:19
  14.5 0.6 copy-done.8
  15.2 0.7 copy-done.7
  15.9 4.1 %all-to-all-done = f32[8,2,2432]{2,1,0:T(2,128)S(1)} async-done(((f32[8,2,2432]{2,1,0:T(2,128)}), f32[8,2,2432]{2,1,0:T(2,128)S(1)}, u32[]{:S(2)}, u32[]{:S(2)}) %all-to-all-start) | async-done | bytes 155680 | tf_op jit(solution)/shard_map/all_to_all | solution.py:19
  20.1 0.7 broadcast_in_dim.60
  20.8 3.4 %all-to-all-start.1 = ((f32[8,2,2432]{2,1,0:T(2,128)}), f32[8,2,2432]{2,1,0:T(2,128)S(1)}, u32[]{:S(2)}, u32[]{:S(2)}) async-start(f32[8,2,2432]{2,1,0:T(2,128)} %broadcast_in_dim.60), calls=%async_computation.1 | async-start | bytes 311296 | tf_op jit(solution)/shard_map/all_to_all | solution.py:24
  24.3 7.8 %all-to-all-done.1 = f32[8,2,2432]{2,1,0:T(2,128)S(1)} async-done(((f32[8,2,2432]{2,1,0:T(2,128)}), f32[8,2,2432]{2,1,0:T(2,128)S(1)}, u32[]{:S(2)}, u32[]{:S(2)}) %all-to-all-start.1) | async-done | bytes 155680 | tf_op jit(solution)/shard_map/all_to_all | solution.py:24
  32.4 0.7 broadcast_in_dim.62
  33.1 5.8 %all-to-all-start.2 = ((f32[8,2,17,128]{3,1,2,0:T(2,128)}), f32[8,2,17,128]{3,1,2,0:T(2,128)S(1)}, u32[]{:S(2)}, u32[]{:S(2)}) async-start(f32[8,2,17,128]{3,1,2,0:T(2,128)} %broadcast_in_dim.62), calls=%async_computation.2 | async-start | bytes 278528 | tf_op jit(solution)/shard_map/all_to_all | solution.py:24
  38.9 5.3 %all-to-all-done.2 = f32[8,2,17,128]{3,1,2,0:T(2,128)S(1)} async-done(((f32[8,2,17,128]{3,1,2,0:T(2,128)}), f32[8,2,17,128]{3,1,2,0:T(2,128)S(1)}, u32[]{:S(2)}, u32[]{:S(2)}) %all-to-all-start.2) | async-done | bytes 139296 | tf_op jit(solution)/shard_map/all_to_all | solution.py:24
  44.3 0.5 select_reduce_fusion.1
  45.0 0.3 fusion.2
  45.4 0.7 copy.152
  46.1 4.2 %all-to-all-start.3 = ((f32[8,2,18,128]{3,1,2,0:T(2,128)}), f32[8,2,18,128]{3,1,2,0:T(2,128)S(1)}, u32[]{:S(2)}, u32[]{:S(2)}) async-start(f32[8,2,18,128]{3,1,2,0:T(2,128)} %copy.152), calls=%async_computation.3 | async-start | bytes 294912 | tf_op jit(solution)/shard_map/all_to_all | solution.py:19
  50.3 5.4 %all-to-all-done.3 = f32[8,2,18,128]{3,1,2,0:T(2,128)S(1)} async-done(((f32[8,2,18,128]{3,1,2,0:T(2,128)}), f32[8,2,18,128]{3,1,2,0:T(2,128)S(1)}, u32[]{:S(2)}, u32[]{:S(2)}) %all-to-all-start.3) | async-done | bytes 147488 | tf_op jit(solution)/shard_map/all_to_all | solution.py:19
  55.9 0.2 fusion.18
  56.1 0.7 broadcast_in_dim.65
  56.8 3.4 %all-to-all-start.4 = ((f32[8,2,18,128]{3,1,2,0:T(2,128)}), f32[8,2,18,128]{3,1,2,0:T(2,128)S(1)}, u32[]{:S(2)}, u32[]{:S(2)}) async-start(f32[8,2,18,128]{3,1,2,0:T(2,128)} %broadcast_in_dim.65), calls=%async_computation.4 | async-start | bytes 294912 | tf_op jit(solution)/shard_map/all_to_all | solution.py:24
  60.4 7.6 %all-to-all-done.4 = f32[8,2,18,128]{3,1,2,0:T(2,128)S(1)} async-done(((f32[8,2,18,128]{3,1,2,0:T(2,128)}), f32[8,2,18,128]{3,1,2,0:T(2,128)S(1)}, u32[]{:S(2)}, u32[]{:S(2)}) %all-to-all-start.4) | async-done | bytes 147488 | tf_op jit(solution)/shard_map/all_to_all | solution.py:24
  68.4 0.2 fusion.17
  68.8 10.2 %all_to_all.70 = f32[8,2,17,128]{3,1,2,0:T(2,128)S(1)} all-to-all(f32[8,2,17,128]{3,1,2,0:T(2,128)S(1)} %broadcast_in_dim.67), channel_id=1, replica_groups=mesh['heads'=8,'y'=8,'x'=4,'core'=2] {'x','core'}, dimensions={0} | all-to-all | bytes 278528 | tf_op jit(solution)/shard_map/all_to_all | solution.py:24
  79.1 0.3 fusion.29
  79.4 16.8 %all_to_all.71 = f32[8,16,256]{2,1,0:T(8,128)S(1)} all-to-all(f32[8,16,256]{2,1,0:T(8,128)S(1)} %broadcast_in_dim.68), channel_id=1, replica_groups=mesh['heads'=8,'y'=8,'x'=4,'core'=2] {'heads'}, dimensions={0} | all-to-all | bytes 262144 | tf_op jit(solution)/shard_map/all_to_all | solution.py:24
  96.4 0.8 copy-done.5
  97.3 0.3 fusion.62
  97.8 10.3 %all_to_all.72 = f32[8,2,2432]{2,1,0:T(2,128)S(1)} all-to-all(f32[8,2,2432]{2,1,0:T(2,128)S(1)} %reshape.246), channel_id=1, replica_groups=mesh['heads'=8,'y'=8,'x'=4,'core'=2] {'x','core'}, dimensions={0} | all-to-all | bytes 311296 | tf_op jit(solution)/shard_map/all_to_all | solution.py:19
  108.2 10.4 %all_to_all.73 = f32[8,2,2432]{2,1,0:T(2,128)S(1)} all-to-all(f32[8,2,2432]{2,1,0:T(2,128)S(1)} %broadcast_in_dim.70), channel_id=1, replica_groups=mesh['heads'=8,'y'=8,'x'=4,'core'=2] {'y'}, dimensions={0} | all-to-all | bytes 311296 | tf_op jit(solution)/shard_map/all_to_all | solution.py:24
  118.9 0.7 broadcast_in_dim.72
  119.6 5.8 %all-to-all-start.9 = ((f32[8,2,17,128]{3,1,2,0:T(2,128)}), f32[8,2,17,128]{3,1,2,0:T(2,128)S(1)}, u32[]{:S(2)}, u32[]{:S(2)}) async-start(f32[8,2,17,128]{3,1,2,0:T(2,128)} %broadcast_in_dim.72), calls=%async_computation.9 | async-start | bytes 278528 | tf_op jit(solution)/shard_map/all_to_all | solution.py:24
  125.3 5.4 %all-to-all-done.9 = f32[8,2,17,128]{3,1,2,0:T(2,128)S(1)} async-done(((f32[8,2,17,128]{3,1,2,0:T(2,128)}), f32[8,2,17,128]{3,1,2,0:T(2,128)S(1)}, u32[]{:S(2)}, u32[]{:S(2)}) %all-to-all-start.9) | async-done | bytes 139296 | tf_op jit(solution)/shard_map/all_to_all | solution.py:24
  130.8 0.5 select_reduce_fusion
  131.5 0.3 fusion
  131.8 0.7 copy.167
  132.6 4.2 %all-to-all-start.10 = ((f32[8,2,18,128]{3,1,2,0:T(2,128)}), f32[8,2,18,128]{3,1,2,0:T(2,128)S(1)}, u32[]{:S(2)}, u32[]{:S(2)}) async-start(f32[8,2,18,128]{3,1,2,0:T(2,128)} %copy.167), calls=%async_computation.10 | async-start | bytes 294912 | tf_op jit(solution)/shard_map/all_to_all | solution.py:19
  136.9 5.3 %all-to-all-done.10 = f32[8,2,18,128]{3,1,2,0:T(2,128)S(1)} async-done(((f32[8,2,18,128]{3,1,2,0:T(2,128)}), f32[8,2,18,128]{3,1,2,0:T(2,128)S(1)}, u32[]{:S(2)}, u32[]{:S(2)}) %all-to-all-start.10) | async-done | bytes 147488 | tf_op jit(solution)/shard_map/all_to_all | solution.py:19
  142.3 0.2 fusion.14
  142.6 0.7 broadcast_in_dim.73
  143.3 3.4 %all-to-all-start.11 = ((f32[8,2,18,128]{3,1,2,0:T(2,128)}), f32[8,2,18,128]{3,1,2,0:T(2,128)S(1)}, u32[]{:S(2)}, u32[]{:S(2)}) async-start(f32[8,2,18,128]{3,1,2,0:T(2,128)} %broadcast_in_dim.73), calls=%async_computation.11 | async-start | bytes 294912 | tf_op jit(solution)/shard_map/all_to_all | solution.py:24
  146.9 7.6 %all-to-all-done.11 = f32[8,2,18,128]{3,1,2,0:T(2,128)S(1)} async-done(((f32[8,2,18,128]{3,1,2,0:T(2,128)}), f32[8,2,18,128]{3,1,2,0:T(2,128)S(1)}, u32[]{:S(2)}, u32[]{:S(2)}) %all-to-all-start.11) | async-done | bytes 147488 | tf_op jit(solution)/shard_map/all_to_all | solution.py:24
  154.7 0.2 fusion.13
  155.2 10.2 %all_to_all.74 = f32[8,2,17,128]{3,1,2,0:T(2,128)S(1)} all-to-all(f32[8,2,17,128]{3,1,2,0:T(2,128)S(1)} %broadcast_in_dim.75), channel_id=1, replica_groups=mesh['heads'=8,'y'=8,'x'=4,'core'=2] {'x','core'}, dimensions={0} | all-to-all | bytes 278528 | tf_op jit(solution)/shard_map/all_to_all | solution.py:24
  165.6 0.3 fusion.26
  165.9 10.1 %all_to_all.75 = f32[8,16,256]{2,1,0:T(8,128)S(1)} all-to-all(f32[8,16,256]{2,1,0:T(8,128)S(1)} %broadcast_in_dim.76), channel_id=1, replica_groups=mesh['heads'=8,'y'=8,'x'=4,'core'=2] {'heads'}, dimensions={0} | all-to-all | bytes 262144 | tf_op jit(solution)/shard_map/all_to_all | solution.py:24
  176.0 0.6 pad_maximum_fusion.4
  (112 shorter events, 4.6 us)
Async XLA Ops:
  0.0 44.3 %copy-start = (bf16[1,16,256,128]{3,2,1,0:T(8,128)(2,1)S(1)}, bf16[1,16,256,128]{3,2,1,0:T(8,128)(2,1)}, u32[]{:S(2)}) copy-start(bf16[1,16,256,128]{3,2,1,0:T(8,128)(2,1)} %param.14) | copy-start | bytes 3145732
  0.0 0.9 copy-start.6
  0.0 0.9 copy-start.9
  4.3 15.7 %all-to-all-start = ((f32[8,2,2432]{2,1,0:T(2,128)}), f32[8,2,2432]{2,1,0:T(2,128)S(1)}, u32[]{:S(2)}, u32[]{:S(2)}) async-start(f32[8,2,2432]{2,1,0:T(2,128)} %reshape.239), calls=%async_computation | async-start | bytes 311296 | tf_op jit(solution)/shard_map/all_to_all | solution.py:19
  14.5 0.7 copy-start.8
  15.2 0.7 copy-start.7
  20.8 11.3 %all-to-all-start.1 = ((f32[8,2,2432]{2,1,0:T(2,128)}), f32[8,2,2432]{2,1,0:T(2,128)S(1)}, u32[]{:S(2)}, u32[]{:S(2)}) async-start(f32[8,2,2432]{2,1,0:T(2,128)} %broadcast_in_dim.60), calls=%async_computation.1 | async-start | bytes 311296 | tf_op jit(solution)/shard_map/all_to_all | solution.py:24
  33.1 11.2 %all-to-all-start.2 = ((f32[8,2,17,128]{3,1,2,0:T(2,128)}), f32[8,2,17,128]{3,1,2,0:T(2,128)S(1)}, u32[]{:S(2)}, u32[]{:S(2)}) async-start(f32[8,2,17,128]{3,1,2,0:T(2,128)} %broadcast_in_dim.62), calls=%async_computation.2 | async-start | bytes 278528 | tf_op jit(solution)/shard_map/all_to_all | solution.py:24
  38.9 6.1 %copy-start.3 = (bf16[1,16,256,128]{3,2,1,0:T(8,128)(2,1)S(1)}, bf16[1,16,256,128]{3,2,1,0:T(8,128)(2,1)}, u32[]{:S(2)}) copy-start(bf16[1,16,256,128]{3,2,1,0:T(8,128)(2,1)} %param.15) | copy-start | bytes 3145732
  46.1 9.6 %all-to-all-start.3 = ((f32[8,2,18,128]{3,1,2,0:T(2,128)}), f32[8,2,18,128]{3,1,2,0:T(2,128)S(1)}, u32[]{:S(2)}, u32[]{:S(2)}) async-start(f32[8,2,18,128]{3,1,2,0:T(2,128)} %copy.152), calls=%async_computation.3 | async-start | bytes 294912 | tf_op jit(solution)/shard_map/all_to_all | solution.py:19
  50.3 28.9 %copy-start.1 = (bf16[2048,256]{1,0:T(8,128)(2,1)S(1)}, bf16[2048,256]{1,0:T(8,128)(2,1)}, u32[]{:S(2)}) copy-start(bf16[2048,256]{1,0:T(8,128)(2,1)} %param.13) | copy-start | bytes 3145732
  56.8 11.2 %all-to-all-start.4 = ((f32[8,2,18,128]{3,1,2,0:T(2,128)}), f32[8,2,18,128]{3,1,2,0:T(2,128)S(1)}, u32[]{:S(2)}, u32[]{:S(2)}) async-start(f32[8,2,18,128]{3,1,2,0:T(2,128)} %broadcast_in_dim.65), calls=%async_computation.4 | async-start | bytes 294912 | tf_op jit(solution)/shard_map/all_to_all | solution.py:24
  79.0 18.3 %copy-start.2 = (bf16[256,2048]{1,0:T(8,128)(2,1)S(1)}, bf16[256,2048]{1,0:T(8,128)(2,1)}, u32[]{:S(2)}) copy-start(bf16[256,2048]{1,0:T(8,128)(2,1)} %param.11) | copy-start | bytes 3145732
  96.3 0.9 copy-start.5
  119.6 11.1 %all-to-all-start.9 = ((f32[8,2,17,128]{3,1,2,0:T(2,128)}), f32[8,2,17,128]{3,1,2,0:T(2,128)S(1)}, u32[]{:S(2)}, u32[]{:S(2)}) async-start(f32[8,2,17,128]{3,1,2,0:T(2,128)} %broadcast_in_dim.72), calls=%async_computation.9 | async-start | bytes 278528 | tf_op jit(solution)/shard_map/all_to_all | solution.py:24
  125.3 6.1 %copy-start.4 = (bf16[1,16,256,128]{3,2,1,0:T(8,128)(2,1)S(1)}, bf16[1,16,256,128]{3,2,1,0:T(8,128)(2,1)}, u32[]{:S(2)}) copy-start(bf16[1,16,256,128]{3,2,1,0:T(8,128)(2,1)} %param.15) | copy-start | bytes 3145732
  132.6 9.6 %all-to-all-start.10 = ((f32[8,2,18,128]{3,1,2,0:T(2,128)}), f32[8,2,18,128]{3,1,2,0:T(2,128)S(1)}, u32[]{:S(2)}, u32[]{:S(2)}) async-start(f32[8,2,18,128]{3,1,2,0:T(2,128)} %copy.167), calls=%async_computation.10 | async-start | bytes 294912 | tf_op jit(solution)/shard_map/all_to_all | solution.py:19
  143.3 11.2 %all-to-all-start.11 = ((f32[8,2,18,128]{3,1,2,0:T(2,128)}), f32[8,2,18,128]{3,1,2,0:T(2,128)S(1)}, u32[]{:S(2)}, u32[]{:S(2)}) async-start(f32[8,2,18,128]{3,1,2,0:T(2,128)} %broadcast_in_dim.73), calls=%async_computation.11 | async-start | bytes 294912 | tf_op jit(solution)/shard_map/all_to_all | solution.py:24

commit v2 on v0

v2 whole, which is shorter than its diff:
```python
import functools
import math

import jax
import jax.numpy as jnp
from jax import lax
from jax.experimental import pallas as pl
from jax.experimental.pallas import tpu as pltpu
from jax.sharding import Mesh, PartitionSpec as P

D = 16384
STEPS = 2
EPSILON = 1e-05
ROPE_BASE = 500000.0
FILLER = -3e38
CHIPS_Y = 8
INNER = ("x", "core")
SEQ = ("y", "x", "core")

ROWS = 16
HEADS = 16
DIM = 128
GROUP = 8
OWN = ROWS // GROUP
PIECE = 40
BATCH = 4
CHUNKS = 4
SCALE = 1.0 / math.sqrt(DIM)
F32 = jnp.float32
BF16 = jnp.bfloat16


def kernel_call(body, out_shapes, *args, scratch=(), space=pltpu.VMEM):
    single = not isinstance(out_shapes, (list, tuple))
    vmem = pl.BlockSpec(memory_space=pltpu.VMEM)
    return pl.pallas_call(
        body,
        out_shape=out_shapes,
        in_specs=[pl.BlockSpec(memory_space=space)] * len(args),
        out_specs=vmem if single else [vmem] * len(out_shapes),
        scratch_shapes=list(scratch),
        compiler_params=pltpu.CompilerParams(vmem_limit_bytes=16 * 1024 * 1024),
    )(*args)


def shape(*dims):
    return jax.ShapeDtypeStruct(dims, F32)


def project(wide, gain_ref, wq_ref, wkv_ref, pieces_ref, waits=None):
    gained = (wide * gain_ref[0:1, :]).astype(BF16)

    def put(row, block):
        for r in range(OWN):
            pieces_ref[pl.ds(row(r), GROUP, stride=PIECE), :] = block[r * GROUP : (r + 1) * GROUP]

    for j in range(HEADS // 2):
        if waits:
            waits[j]()
        both = jnp.dot(gained, wq_ref[:, 2 * j * DIM : 2 * (j + 1) * DIM], preferred_element_type=F32)
        for k in range(2):
            put(lambda r: r * HEADS + 2 * j + k, both[:, k * DIM : (k + 1) * DIM])
    if waits:
        waits[-1]()
    both = jnp.dot(gained, wkv_ref[...], preferred_element_type=F32)
    put(lambda r: 2 * HEADS + r, both[:, :DIM])
    put(lambda r: 2 * HEADS + OWN + r, both[:, DIM:])
    squares = jnp.broadcast_to(jnp.sum(wide * wide, axis=1, keepdims=True), (ROWS, DIM))
    put(lambda r: 2 * HEADS + 2 * OWN + r, squares)
    put(lambda r: 2 * HEADS + 3 * OWN + r, jnp.zeros((ROWS, DIM), F32))


def first_kernel(
    tokens_hbm, gain_hbm, wq_hbm, wkv_hbm, lengths_hbm, positions_hbm,
    pieces_ref, wide_ref, gain_ref, seen_ref, *refs,
):
    table_refs, (tokens_ref, gain_in, wq_ref, wkv_ref, lengths_ref, positions_ref, left_ref, right_ref, sems) = (
        refs[:STEPS], refs[STEPS:],
    )
    chunk = wq_ref.shape[1] // CHUNKS
    pairs = [
        (lengths_hbm, lengths_ref),
        (positions_hbm, positions_ref),
        (tokens_hbm, tokens_ref),
        (gain_hbm, gain_in),
        (wkv_hbm, wkv_ref),
    ]
    columns = [pl.ds(c * chunk, chunk) for c in range(CHUNKS)]
    pairs += [(wq_hbm.at[:, c], wq_ref.at[:, c]) for c in columns]
    copies = [pltpu.make_async_copy(a, b, sems.at[i]) for i, (a, b) in enumerate(pairs)]
    for copy in copies:
        copy.start()
    inner = lax.axis_index("x") * 2 + lax.axis_index("core")
    seq_here = seen_ref.shape[1]
    spot = (lax.axis_index("y") * GROUP + inner) * seq_here + lax.broadcasted_iota(jnp.int32, (1, seq_here), 1)
    copies[0].wait()
    copies[1].wait()
    for b in range(ROWS):
        seen_ref[b : b + 1, :] = jnp.where(spot < lengths_ref[b], 1.0, 0.0)
    lane = lax.broadcasted_iota(jnp.int32, (8, DIM), 1)
    line = lax.broadcasted_iota(jnp.int32, (8, DIM), 0)
    index = jnp.where(lane < DIM // 2, lane, lane - DIM // 2).astype(F32)
    freqs = jnp.exp(index * (-2.0 * math.log(ROPE_BASE) / DIM))
    place = jnp.where(line % 2 == 1, positions_ref[inner * OWN + 1], positions_ref[inner * OWN])
    for step, ref in enumerate(table_refs):
        angles = (place + step).astype(F32) * freqs
        sine = jnp.sin(angles)
        ref[...] = jnp.where(line < OWN, jnp.cos(angles), jnp.where(lane < DIM // 2, -sine, sine))
    copies[2].wait()
    copies[3].wait()
    width = tokens_ref.shape[1] // 2
    left_ref[...] = tokens_ref[:, :width].astype(F32)
    right_ref[...] = tokens_ref[:, width:].astype(F32)
    wide = jnp.concatenate(
        [
            jnp.concatenate([ref[pl.ds(r, GROUP, stride=OWN), :] for r in range(OWN)], axis=0)
            for ref in (left_ref, right_ref)
        ],
        axis=1,
    )
    wide_ref[...] = wide
    gain_ref[...] = jnp.broadcast_to(gain_in[...].astype(F32).reshape(1, 2 * width), gain_ref.shape)
    waits = [lambda j=j: copies[5 + j * 2 * DIM // chunk].wait() if j * 2 * DIM % chunk == 0 else None for j in range(HEADS // 2)]
    project(wide, gain_ref, wq_ref, wkv_ref, pieces_ref, waits + [copies[4].wait])


def next_kernel(sums_ref, last_ref, gain_ref, wq_ref, wkv_ref, pieces_ref, output_ref):
    output = sums_ref[0]
    for s in range(1, GROUP):
        output = output + sums_ref[s]
    output_ref[...] = output
    wide = (last_ref[...] + output).astype(BF16).astype(F32)
    project(wide, gain_ref, wq_ref, wkv_ref, pieces_ref)


def last_kernel(sums_ref, first_ref, result_ref):
    output = sums_ref[0]
    for s in range(1, GROUP):
        output = output + sums_ref[s]
    for step, value in enumerate((first_ref[...], output)):
        for b in range(ROWS):
            at = b % OWN * GROUP + b // OWN
            result_ref[step, b : b + 1, :] = value[at : at + 1, :]


def turn_kernel(parts_ref, table_ref, pieces_ref, own_ref):
    whole = parts_ref[0]
    for s in range(1, GROUP):
        whole = whole + parts_ref[s]
    table = table_ref[...]
    below = whole[2 * HEADS :]
    first = 2 * OWN
    inverse = [lax.rsqrt(below[first + r : first + r + 1] / D + EPSILON) for r in range(OWN)]
    cosine = [table[r : r + 1] for r in range(OWN)]
    sine = [table[OWN + r : OWN + r + 1] for r in range(OWN)]
    blocks = []
    for r in range(OWN):
        scaled = whole[r * HEADS : (r + 1) * HEADS] * inverse[r]
        blocks.append(scaled * cosine[r] + pltpu.roll(scaled, DIM // 2, 1) * sine[r])
    line = lax.broadcasted_iota(jnp.int32, below.shape, 0)
    odd = line % 2 == 1
    scaled = below * jnp.where(odd, inverse[1], inverse[0])
    cosines = jnp.where(line < OWN, jnp.where(odd, cosine[1], cosine[0]), 1.0)
    sines = jnp.where(line < OWN, jnp.where(odd, sine[1], sine[0]), 0.0)
    blocks.append(scaled * cosines + pltpu.roll(scaled, DIM // 2, 1) * sines)
    piece = jnp.concatenate(blocks, axis=0)
    own_ref[...] = piece
    for d in range(GROUP):
        pieces_ref[d] = piece


def diagonal():
    shape_here = (2 * HEADS, DIM)
    return lax.broadcasted_iota(jnp.int32, shape_here, 0) == lax.broadcasted_iota(jnp.int32, shape_here, 1)


def to_lanes(column):
    return jnp.sum(jnp.where(diagonal(), column, 0.0), axis=0, keepdims=True)


def to_column(line):
    return jnp.sum(jnp.where(diagonal(), line, 0.0), axis=1, keepdims=True)


def stats_block(top, total):
    line = lax.broadcasted_iota(jnp.int32, (PIECE - 2 * HEADS, DIM), 0)
    return jnp.where(line == 0, top, jnp.where(line == 1, total, 0.0))


def attend_kernel(queries_ref, keys_ref, values_ref, seen_ref, pieces_ref, work_ref):
    def place(b):
        return b // OWN, slice(b % OWN * HEADS, (b % OWN + 1) * HEADS)

    for b in range(ROWS):
        d, heads = place(b)
        queries = queries_ref[d, heads, :].astype(BF16)
        work_ref[b] = lax.dot_general(queries, keys_ref[b], (((1,), (1,)), ((), ())), preferred_element_type=F32)
    for c in range(0, ROWS, BATCH):
        scores = work_ref[c : c + BATCH] * SCALE
        seen = jnp.broadcast_to(seen_ref[c : c + BATCH, :][:, None, :], scores.shape) > 0.0
        tops = jnp.max(jnp.where(seen, scores, FILLER), axis=2, keepdims=True)
        probs = jnp.where(seen, jnp.exp(scores - tops), 0.0)
        totals = jnp.sum(probs, axis=2, keepdims=True)
        work_ref[c : c + BATCH] = probs
        for b in range(0, BATCH, OWN):
            top = tops[b : b + OWN].reshape(OWN * HEADS, 1)
            total = totals[b : b + OWN].reshape(OWN * HEADS, 1)
            pieces_ref[(c + b) // OWN, 2 * HEADS :, :] = stats_block(to_lanes(top), to_lanes(total))
    for b in range(ROWS):
        d, heads = place(b)
        pieces_ref[d, heads, :] = jnp.dot(work_ref[b].astype(BF16), values_ref[b], preferred_element_type=F32)


def merge(parts_ref):
    tops = [parts_ref[s, 2 * HEADS : 2 * HEADS + 1, :] for s in range(GROUP)]
    top = functools.reduce(jnp.maximum, tops)
    total, weighted = None, None
    for s in range(GROUP):
        factor = jnp.exp(tops[s] - top)
        here = factor * parts_ref[s, 2 * HEADS + 1 : 2 * HEADS + 2, :]
        part = to_column(factor) * parts_ref[s, : 2 * HEADS, :]
        total = here if total is None else total + here
        weighted = part if weighted is None else weighted + part
    return top, total, weighted


def merge_kernel(parts_ref, pieces_ref):
    top, total, weighted = merge(parts_ref)
    stats = stats_block(top, total)
    for d in range(GROUP):
        pieces_ref[d, : 2 * HEADS, :] = weighted
        pieces_ref[d, 2 * HEADS :, :] = stats


def finish_kernel(parts_ref, *refs):
    own_refs, pieces_ref = refs[:-1], refs[-1]

    def rounded(value):
        return value.astype(BF16).astype(F32)

    def spread(ref, line):
        return jnp.concatenate(
            [jnp.broadcast_to(rounded(ref[line + r : line + r + 1, :]), (HEADS, DIM)) for r in range(OWN)], axis=0
        )

    top, total, weighted = merge(parts_ref)
    top, total = to_column(top), to_column(total)
    queries = rounded(own_refs[-1][: 2 * HEADS, :])
    scores = [jnp.sum(queries * spread(ref, 2 * HEADS), axis=1, keepdims=True) * SCALE for ref in own_refs]
    whole_top = functools.reduce(jnp.maximum, scores, top)
    factor = jnp.exp(top - whole_top)
    total = total * factor
    weighted = weighted * factor
    for score, ref in zip(scores, own_refs):
        prob = jnp.exp(score - whole_top)
        total = total + prob
        weighted = weighted + rounded(prob) * spread(ref, 2 * HEADS + OWN)
    attended = weighted / total
    for d in range(GROUP):
        pieces_ref[d] = attended


def out_kernel(attended_ref, wout_ref, pieces_ref):
    partial = None
    for j in range(HEADS // 2):
        heads = jnp.concatenate(
            [
                jnp.concatenate(
                    [attended_ref[pl.ds(r * HEADS + 2 * j + k, GROUP, stride=2 * HEADS), :] for r in range(OWN)], axis=0
                )
                for k in range(2)
            ],
            axis=1,
        ).astype(BF16)
        term = jnp.dot(heads, wout_ref[2 * j * DIM : 2 * (j + 1) * DIM, :], preferred_element_type=F32)
        partial = term if partial is None else partial + term
    for d in range(GROUP):
        pieces_ref[d] = partial


def exchange(pieces, axes):
    return lax.all_to_all(pieces, axes, 0, 0, tiled=True)


def per_device(tokens, norm_gain, w_query, w_kv, w_out, key_cache, value_cache, lengths, positions):
    seq_here = key_cache.shape[2]
    width = tokens.shape[1]
    keys, values = key_cache[0], value_cache[0]
    flat = shape(GROUP * PIECE, DIM)
    cube = shape(GROUP, PIECE, DIM)
    half = pltpu.VMEM((ROWS, width // 2), F32)
    work = pltpu.VMEM((ROWS, HEADS, seq_here), F32)
    line = shape(8, DIM)
    pieces, wide, gain, seen, *tables = kernel_call(
        first_kernel,
        [flat, shape(ROWS, width), shape(8, width), shape(ROWS, seq_here)] + [line] * STEPS,
        *[
            pltpu.with_memory_space_constraint(array, pltpu.HBM)
            for array in (tokens, norm_gain, w_query, w_kv, lengths, positions)
        ],
        scratch=[
            pltpu.VMEM(tokens.shape, BF16),
            pltpu.VMEM(norm_gain.shape, BF16),
            pltpu.VMEM(w_query.shape, BF16),
            pltpu.VMEM(w_kv.shape, BF16),
            pltpu.SMEM(lengths.shape, jnp.int32),
            pltpu.SMEM(positions.shape, jnp.int32),
            half,
            half,
            pltpu.SemaphoreType.DMA((5 + CHUNKS,)),
        ],
        space=pltpu.HBM,
    )
    own, output = [], None
    for step in range(STEPS):
        if step:
            pieces, output = kernel_call(
                next_kernel, [flat, shape(ROWS, width)], sums, wide, gain, w_query, w_kv
            )
        parts = exchange(pieces.reshape(GROUP, PIECE, DIM), INNER)
        total = jnp.broadcast_to(jnp.sum(parts, axis=0)[None], (GROUP, PIECE, DIM))
        parts = exchange(total, ("y",))
        pieces, mine = kernel_call(turn_kernel, [cube, shape(PIECE, DIM)], parts, tables[step])
        own.append(mine)
        queries = exchange(pieces, INNER)
        parts = exchange(kernel_call(attend_kernel, cube, queries, keys, values, seen, scratch=[work]), INNER)
        parts = exchange(kernel_call(merge_kernel, cube, parts), ("y",))
        pieces = kernel_call(finish_kernel, shape(GROUP, 2 * HEADS, DIM), parts, *own)
        attended = exchange(pieces, INNER).reshape(GROUP * 2 * HEADS, DIM)
        sums = exchange(kernel_call(out_kernel, shape(GROUP, ROWS, width), attended, w_out), ("heads",))
    return kernel_call(last_kernel, shape(STEPS, ROWS, width), sums, output)


def solution(mesh):
    heads_size, seq_size = mesh.shape["heads"], mesh.shape["seq"]
    devices = mesh.devices.reshape(heads_size, CHIPS_Y, seq_size // CHIPS_Y // 2, 2)
    fine = Mesh(devices, ("heads", "y", "x", "core"))
    in_specs = (
        P(None, SEQ),
        P(SEQ),
        P(SEQ, "heads"),
        P(SEQ, "heads"),
        P("heads", SEQ),
        P("heads", None, SEQ, None),
        P("heads", None, SEQ, None),
        P(),
        P(),
    )
    return jax.shard_map(
        per_device, mesh=fine, in_specs=in_specs, out_specs=P(None, None, SEQ), check_vma=False
    )
```

time: 1640 us -> 162 us (0.10)
  blocking collectives: 1050 us -> 156 us
  waiting for transfers between devices: 548 us -> 0 us
    psum x6 -> x0, blocking collectives: 796 us -> none  [the longest x2 494 us: per_device(): lax.psum((jnp.sum(wide * wide, axis=1), jnp.dot(gained, w_query, preferre...]
    psum x4 -> x0, waiting for transfers between devices: 548 us -> none  [the longest x2 365 us: per_device(): total, weighted = lax.psum((jnp.sum(probs, axis=-1), weighted), 'seq')]
    pmax x2 -> x0, blocking collectives: 256 us -> none  [per_device(): lax.pmax(local_top, 'seq')]
    all_to_all x0 -> x14, blocking collectives: none -> 156 us  [exchange(): return lax.all_to_all(pieces, axes, 0, 0, tiled=True)]
  transfers between devices with their start and end apart: 4 -> 0, of which waited for: 3 -> 0; matrix products, arithmetic and copies ran while one was open for 0% -> 0% of each run, Pallas kernels for 0% -> 0%
where the time goes in v2:
time: 162 us; the launch traced here: 161 us
  blocking collectives  156 us (96%)
  Pallas kernels  5.32 us (3%)
    all_to_all x14, blocking collectives, exchange(): return lax.all_to_all(pieces, axes, 0, 0, tiled=True)  156 us
    pallas_call x13, Pallas kernels, kernel_call(): pl.pallas_call(body, out_shape=out_shapes, in_specs=[pl.BlockSpec(memory_...  5.32 us

profile of v2, /device:TPU:1, one launch (start us, length us, event | category | flops | bytes accessed | tf_op | source)
XLA Modules:
  0.0 161.1 jit_solution(1170919701667246872)
XLA Ops:
  0.0 0.0 copy-start.1
  0.0 2.0 %shard_map.91 = (f32[320,128]{1,0:T(8,128)S(1)}, f32[16,256]{1,0:T(8,128)S(1)}, f32[8,256]{1,0:T(8,128)S(1)}, f32[16,256]{1,0:T(8,128)S(1)}, f32[8,128]{1,0:T(8,128)S(1)}, /*index=5*/f32[8,128]{1,0:T(8,128)S(1)}) custom-call(bf16[16,256]{1,0:T(8,128)(2,1)} %tokens_hbm.1, bf16[256]{0:T(256)(128)(2,1)} %gain_hbm.1, bf16[256,2048]{1,0:T(8,128)(2,1)} %wq_ref.1, ...), custom_call_target="tpu_custom_call" | custom-call | tf_op jit(solution)/shard_map/pallas_call | solution.py:36
  2.0 0.0 copy-start
  2.0 15.0 %all_to_all.70 = f32[8,40,128]{2,1,0:T(8,128)S(1)} all-to-all(f32[8,40,128]{2,1,0:T(8,128)S(1)} %bitcast.12), channel_id=1, replica_groups=mesh['heads'=8,'y'=8,'x'=4,'core'=2] {'x','core'}, dimensions={0} | all-to-all | bytes 327680 | tf_op jit(solution)/shard_map/all_to_all | solution.py:282
  17.0 11.0 %all_to_all.71.parts_ref = f32[8,40,128]{2,1,0:T(8,128)S(1)} all-to-all(f32[8,40,128]{2,1,0:T(8,128)S(1)} %broadcast_in_dim.4), channel_id=1, replica_groups=mesh['heads'=8,'y'=8,'x'=4,'core'=2] {'y'}, dimensions={0} | all-to-all | bytes 327680 | tf_op jit(solution)/shard_map/all_to_all | solution.py:282
  28.0 0.1 shard_map.92
  28.1 10.6 %all_to_all.72.queries_ref = f32[8,40,128]{2,1,0:T(8,128)S(1)} all-to-all(f32[8,40,128]{2,1,0:T(8,128)S(1)} %get-tuple-element.19), channel_id=1, replica_groups=mesh['heads'=8,'y'=8,'x'=4,'core'=2] {'x','core'}, dimensions={0} | all-to-all | bytes 327680 | tf_op jit(solution)/shard_map/all_to_all | solution.py:282
  38.8 0.0 copy-done.1
  38.8 0.0 copy-done
  38.8 0.6 shard_map.93
  39.4 0.0 copy-start.2
  39.4 9.0 %all_to_all.73.parts_ref = f32[8,40,128]{2,1,0:T(8,128)S(1)} all-to-all(f32[8,40,128]{2,1,0:T(8,128)S(1)} %shard_map.93), channel_id=1, replica_groups=mesh['heads'=8,'y'=8,'x'=4,'core'=2] {'x','core'}, dimensions={0} | all-to-all | bytes 327680 | tf_op jit(solution)/shard_map/all_to_all | solution.py:282
  48.4 0.1 shard_map.94
  48.5 10.6 %all_to_all.74.parts_ref = f32[8,40,128]{2,1,0:T(8,128)S(1)} all-to-all(f32[8,40,128]{2,1,0:T(8,128)S(1)} %shard_map.94), channel_id=1, replica_groups=mesh['heads'=8,'y'=8,'x'=4,'core'=2] {'y'}, dimensions={0} | all-to-all | bytes 327680 | tf_op jit(solution)/shard_map/all_to_all | solution.py:282
  59.1 0.0 copy-start.3
  59.1 0.1 shard_map.95
  59.3 10.3 %all_to_all.75 = f32[8,32,128]{2,1,0:T(8,128)S(1)} all-to-all(f32[8,32,128]{2,1,0:T(8,128)S(1)} %shard_map.95), channel_id=1, replica_groups=mesh['heads'=8,'y'=8,'x'=4,'core'=2] {'x','core'}, dimensions={0} | all-to-all | bytes 262144 | tf_op jit(solution)/shard_map/all_to_all | solution.py:282
  69.6 0.0 copy-done.2
  69.6 0.3 shard_map.96
  69.8 0.0 copy-start.4
  69.8 17.8 %all_to_all.76.sums_ref = f32[8,16,256]{2,1,0:T(8,128)S(1)} all-to-all(f32[8,16,256]{2,1,0:T(8,128)S(1)} %shard_map.96), channel_id=1, replica_groups=mesh['heads'=8,'y'=8,'x'=4,'core'=2] {'heads'}, dimensions={0} | all-to-all | bytes 262144 | tf_op jit(solution)/shard_map/all_to_all | solution.py:282
  87.7 0.0 copy-done.3
  87.7 0.0 copy-done.4
  87.7 0.3 shard_map.97
  87.9 10.3 %all_to_all.77 = f32[8,40,128]{2,1,0:T(8,128)S(1)} all-to-all(f32[8,40,128]{2,1,0:T(8,128)S(1)} %bitcast.13), channel_id=1, replica_groups=mesh['heads'=8,'y'=8,'x'=4,'core'=2] {'x','core'}, dimensions={0} | all-to-all | bytes 327680 | tf_op jit(solution)/shard_map/all_to_all | solution.py:282
  98.3 10.6 %all_to_all.78.parts_ref = f32[8,40,128]{2,1,0:T(8,128)S(1)} all-to-all(f32[8,40,128]{2,1,0:T(8,128)S(1)} %broadcast_in_dim.5), channel_id=1, replica_groups=mesh['heads'=8,'y'=8,'x'=4,'core'=2] {'y'}, dimensions={0} | all-to-all | bytes 327680 | tf_op jit(solution)/shard_map/all_to_all | solution.py:282
  108.9 0.1 shard_map.98
  109.0 10.5 %all_to_all.79.queries_ref = f32[8,40,128]{2,1,0:T(8,128)S(1)} all-to-all(f32[8,40,128]{2,1,0:T(8,128)S(1)} %get-tuple-element.26), channel_id=1, replica_groups=mesh['heads'=8,'y'=8,'x'=4,'core'=2] {'x','core'}, dimensions={0} | all-to-all | bytes 327680 | tf_op jit(solution)/shard_map/all_to_all | solution.py:282
  119.5 0.6 shard_map.99
  120.1 8.9 %all_to_all.80.parts_ref = f32[8,40,128]{2,1,0:T(8,128)S(1)} all-to-all(f32[8,40,128]{2,1,0:T(8,128)S(1)} %shard_map.99), channel_id=1, replica_groups=mesh['heads'=8,'y'=8,'x'=4,'core'=2] {'x','core'}, dimensions={0} | all-to-all | bytes 327680 | tf_op jit(solution)/shard_map/all_to_all | solution.py:282
  129.0 0.1 shard_map.100
  129.1 10.6 %all_to_all.81.parts_ref = f32[8,40,128]{2,1,0:T(8,128)S(1)} all-to-all(f32[8,40,128]{2,1,0:T(8,128)S(1)} %shard_map.100), channel_id=1, replica_groups=mesh['heads'=8,'y'=8,'x'=4,'core'=2] {'y'}, dimensions={0} | all-to-all | bytes 327680 | tf_op jit(solution)/shard_map/all_to_all | solution.py:282
  139.7 0.1 shard_map.101
  139.8 10.2 %all_to_all.82 = f32[8,32,128]{2,1,0:T(8,128)S(1)} all-to-all(f32[8,32,128]{2,1,0:T(8,128)S(1)} %shard_map.101), channel_id=1, replica_groups=mesh['heads'=8,'y'=8,'x'=4,'core'=2] {'x','core'}, dimensions={0} | all-to-all | bytes 262144 | tf_op jit(solution)/shard_map/all_to_all | solution.py:282
  150.0 0.3 shard_map.102
  150.3 10.1 %all_to_all.83.sums_ref = f32[8,16,256]{2,1,0:T(8,128)S(1)} all-to-all(f32[8,16,256]{2,1,0:T(8,128)S(1)} %shard_map.102), channel_id=1, replica_groups=mesh['heads'=8,'y'=8,'x'=4,'core'=2] {'heads'}, dimensions={0} | all-to-all | bytes 262144 | tf_op jit(solution)/shard_map/all_to_all | solution.py:282
  160.4 0.6 shard_map.103
  (4 shorter events, 0.1 us)
Async XLA Ops:
  0.0 38.8 %copy-start.1 = (bf16[1,16,256,128]{3,2,1,0:T(8,128)(2,1)S(1)}, bf16[1,16,256,128]{3,2,1,0:T(8,128)(2,1)}, u32[]{:S(2)}) copy-start(bf16[1,16,256,128]{3,2,1,0:T(8,128)(2,1)} %param.15) | copy-start | bytes 3145732
  2.0 36.8 %copy-start = (bf16[1,16,256,128]{3,2,1,0:T(8,128)(2,1)S(1)}, bf16[1,16,256,128]{3,2,1,0:T(8,128)(2,1)}, u32[]{:S(2)}) copy-start(bf16[1,16,256,128]{3,2,1,0:T(8,128)(2,1)} %param.14) | copy-start | bytes 3145732
  39.4 30.2 %copy-start.2 = (bf16[2048,256]{1,0:T(8,128)(2,1)S(1)}, bf16[2048,256]{1,0:T(8,128)(2,1)}, u32[]{:S(2)}) copy-start(bf16[2048,256]{1,0:T(8,128)(2,1)} %wout_ref.3) | copy-start | bytes 3145732
  59.1 28.5 %copy-start.3 = (bf16[256,2048]{1,0:T(8,128)(2,1)S(1)}, bf16[256,2048]{1,0:T(8,128)(2,1)}, u32[]{:S(2)}) copy-start(bf16[256,2048]{1,0:T(8,128)(2,1)} %wq_ref.1) | copy-start | bytes 3145732
  69.8 17.8 %copy-start.4 = (bf16[256,256]{1,0:T(8,128)(2,1)S(1)}, bf16[256,256]{1,0:T(8,128)(2,1)}, u32[]{:S(2)}) copy-start(bf16[256,256]{1,0:T(8,128)(2,1)} %wkv_ref.1) | copy-start | bytes 393220

commit v3 on v2

--- a/solution.py
+++ b/solution.py
@@ -23,14 +23,21 @@
 GROUP = 8
 OWN = ROWS // GROUP
 PIECE = 40
-BATCH = 4
+BATCH = 2
 CHUNKS = 4
 SCALE = 1.0 / math.sqrt(DIM)
 F32 = jnp.float32
 BF16 = jnp.bfloat16
 
 
-def kernel_call(body, out_shapes, *args, scratch=(), space=pltpu.VMEM):
+def kernel_call(body, out_shapes, *args, scratch=(), space=pltpu.VMEM, after=()):
+    count = len(args)
+    if after:
+        inner, args = body, args + tuple(after)
+
+        def body(*refs):
+            inner(*refs[:count], *refs[len(args) :])
+
     single = not isinstance(out_shapes, (list, tuple))
     vmem = pl.BlockSpec(memory_space=pltpu.VMEM)
     return pl.pallas_call(
@@ -45,6 +52,10 @@
 
 def shape(*dims):
     return jax.ShapeDtypeStruct(dims, F32)
+
+
+def core_row(i, core):
+    return i // OWN * (2 * OWN) + core * OWN + i % OWN
 
 
 def project(wide, gain_ref, wq_ref, wkv_ref, pieces_ref, waits=None):
@@ -91,12 +102,17 @@
     for copy in copies:
         copy.start()
     inner = lax.axis_index("x") * 2 + lax.axis_index("core")
-    seq_here = seen_ref.shape[1]
-    spot = (lax.axis_index("y") * GROUP + inner) * seq_here + lax.broadcasted_iota(jnp.int32, (1, seq_here), 1)
+    core = lax.axis_index("core")
+    seq_here = seen_ref.shape[1] // 2
+    column = lax.broadcasted_iota(jnp.int32, (1, 2 * seq_here), 1)
+    block = lax.axis_index("y") * GROUP + lax.axis_index("x") * 2
+    spot = jnp.where(
+        column < seq_here, (block + core) * seq_here + column, (block - core) * seq_here + column
+    )
     copies[0].wait()
     copies[1].wait()
-    for b in range(ROWS):
-        seen_ref[b : b + 1, :] = jnp.where(spot < lengths_ref[b], 1.0, 0.0)
+    for i in range(ROWS // 2):
+        seen_ref[i : i + 1, :] = jnp.where(spot < lengths_ref[core_row(i, core)], 1.0, 0.0)
     lane = lax.broadcasted_iota(jnp.int32, (8, DIM), 1)
     line = lax.broadcasted_iota(jnp.int32, (8, DIM), 0)
     index = jnp.where(lane < DIM // 2, lane, lane - DIM // 2).astype(F32)
@@ -165,8 +181,8 @@
     blocks.append(scaled * cosines + pltpu.roll(scaled, DIM // 2, 1) * sines)
     piece = jnp.concatenate(blocks, axis=0)
     own_ref[...] = piece
-    for d in range(GROUP):
-        pieces_ref[d] = piece
+    for d in range(pieces_ref.shape[0]):
+        pieces_ref[d] = piece[: 2 * HEADS]
 
 
 def diagonal():
@@ -187,15 +203,30 @@
     return jnp.where(line == 0, top, jnp.where(line == 1, total, 0.0))
 
 
-def attend_kernel(queries_ref, keys_ref, values_ref, seen_ref, pieces_ref, work_ref):
-    def place(b):
-        return b // OWN, slice(b % OWN * HEADS, (b % OWN + 1) * HEADS)
-
-    for b in range(ROWS):
-        d, heads = place(b)
-        queries = queries_ref[d, heads, :].astype(BF16)
-        work_ref[b] = lax.dot_general(queries, keys_ref[b], (((1,), (1,)), ((), ())), preferred_element_type=F32)
-    for c in range(0, ROWS, BATCH):
+def swap_kernel(keys_ref, values_ref, other_ref):
+    core = lax.axis_index("core")
+    for i in range(ROWS // 2):
+        b = core_row(i, 1 - core)
+        other_ref[0, i] = keys_ref[b].astype(F32)
+        other_ref[1, i] = values_ref[b].astype(F32)
+
+
+def attend_kernel(queries_ref, keys_ref, values_ref, other_ref, seen_ref, pieces_ref, work_ref):
+    core = lax.axis_index("core")
+    seq_here = keys_ref.shape[1]
+    halves = (slice(0, seq_here), slice(seq_here, 2 * seq_here))
+
+    def place(i):
+        return i // OWN, slice(i % OWN * HEADS, (i % OWN + 1) * HEADS)
+
+    for i in range(ROWS // 2):
+        x, heads = place(i)
+        queries = queries_ref[x, heads, :].astype(BF16)
+        for half, keys in zip(halves, (keys_ref[core_row(i, core)], other_ref[0, i].astype(BF16))):
+            work_ref[i, :, half] = lax.dot_general(
+                queries, keys, (((1,), (1,)), ((), ())), preferred_element_type=F32
+            )
+    for c in range(0, ROWS // 2, BATCH):
         scores = work_ref[c : c + BATCH] * SCALE
         seen = jnp.broadcast_to(seen_ref[c : c + BATCH, :][:, None, :], scores.shape) > 0.0
         tops = jnp.max(jnp.where(seen, scores, FILLER), axis=2, keepdims=True)
@@ -206,16 +237,19 @@
             top = tops[b : b + OWN].reshape(OWN * HEADS, 1)
             total = totals[b : b + OWN].reshape(OWN * HEADS, 1)
             pieces_ref[(c + b) // OWN, 2 * HEADS :, :] = stats_block(to_lanes(top), to_lanes(total))
-    for b in range(ROWS):
-        d, heads = place(b)
-        pieces_ref[d, heads, :] = jnp.dot(work_ref[b].astype(BF16), values_ref[b], preferred_element_type=F32)
+    for i in range(ROWS // 2):
+        x, heads = place(i)
+        own, other = (work_ref[i, :, half].astype(BF16) for half in halves)
+        pieces_ref[x, heads, :] = jnp.dot(
+            own, values_ref[core_row(i, core)], preferred_element_type=F32
+        ) + jnp.dot(other, other_ref[1, i].astype(BF16), preferred_element_type=F32)
 
 
 def merge(parts_ref):
-    tops = [parts_ref[s, 2 * HEADS : 2 * HEADS + 1, :] for s in range(GROUP)]
+    tops = [parts_ref[s, 2 * HEADS : 2 * HEADS + 1, :] for s in range(parts_ref.shape[0])]
     top = functools.reduce(jnp.maximum, tops)
     total, weighted = None, None
-    for s in range(GROUP):
+    for s in range(parts_ref.shape[0]):
         factor = jnp.exp(tops[s] - top)
         here = factor * parts_ref[s, 2 * HEADS + 1 : 2 * HEADS + 2, :]
         part = to_column(factor) * parts_ref[s, : 2 * HEADS, :]
@@ -289,11 +323,11 @@
     flat = shape(GROUP * PIECE, DIM)
     cube = shape(GROUP, PIECE, DIM)
     half = pltpu.VMEM((ROWS, width // 2), F32)
-    work = pltpu.VMEM((ROWS, HEADS, seq_here), F32)
+    work = pltpu.VMEM((ROWS // 2, HEADS, 2 * seq_here), F32)
     line = shape(8, DIM)
     pieces, wide, gain, seen, *tables = kernel_call(
         first_kernel,
-        [flat, shape(ROWS, width), shape(8, width), shape(ROWS, seq_here)] + [line] * STEPS,
+        [flat, shape(ROWS, width), shape(8, width), shape(ROWS // 2, 2 * seq_here)] + [line] * STEPS,
         *[
             pltpu.with_memory_space_constraint(array, pltpu.HBM)
             for array in (tokens, norm_gain, w_query, w_kv, lengths, positions)
@@ -315,19 +349,27 @@
     for step in range(STEPS):
         if step:
             pieces, output = kernel_call(
-                next_kernel, [flat, shape(ROWS, width)], sums, wide, gain, w_query, w_kv
+                next_kernel, [flat, shape(ROWS, width)], sums, wide, gain, w_query, w_kv, after=(other,)
             )
         parts = exchange(pieces.reshape(GROUP, PIECE, DIM), INNER)
         total = jnp.broadcast_to(jnp.sum(parts, axis=0)[None], (GROUP, PIECE, DIM))
         parts = exchange(total, ("y",))
-        pieces, mine = kernel_call(turn_kernel, [cube, shape(PIECE, DIM)], parts, tables[step])
+        if not step:
+            other = kernel_call(swap_kernel, shape(2, ROWS // 2, seq_here, DIM), keys, values, after=(parts,))
+            parts, other = lax.optimization_barrier((parts, other))
+            other = lax.ppermute(other, "core", [(0, 1), (1, 0)])
+        pieces, mine = kernel_call(turn_kernel, [shape(GROUP // 2, 2 * HEADS, DIM), shape(PIECE, DIM)], parts, tables[step], after=(other,) if step else ())
         own.append(mine)
-        queries = exchange(pieces, INNER)
-        parts = exchange(kernel_call(attend_kernel, cube, queries, keys, values, seen, scratch=[work]), INNER)
-        parts = exchange(kernel_call(merge_kernel, cube, parts), ("y",))
-        pieces = kernel_call(finish_kernel, shape(GROUP, 2 * HEADS, DIM), parts, *own)
+        queries = exchange(pieces, ("x",))
+        pieces = kernel_call(
+            attend_kernel, shape(GROUP // 2, PIECE, DIM), queries, keys, values, other, seen, scratch=[work]
+        )
+        parts = exchange(pieces, ("x",))
+        kept = () if step else (other,)
+        parts = exchange(kernel_call(merge_kernel, cube, parts, after=kept), ("y",))
+        pieces = kernel_call(finish_kernel, shape(GROUP, 2 * HEADS, DIM), parts, *own, after=kept)
         attended = exchange(pieces, INNER).reshape(GROUP * 2 * HEADS, DIM)
-        sums = exchange(kernel_call(out_kernel, shape(GROUP, ROWS, width), attended, w_out), ("heads",))
+        sums = exchange(kernel_call(out_kernel, shape(GROUP, ROWS, width), attended, w_out, after=kept), ("heads",))
     return kernel_call(last_kernel, shape(STEPS, ROWS, width), sums, output)
 
 

time: 162 us -> 160 us (0.988)
  blocking collectives: 156 us -> 149 us
  starting transfers between devices: 0 us -> 4.7 us
    all_to_all x14, blocking collectives: 156 us -> 149 us  [exchange(): return lax.all_to_all(pieces, axes, 0, 0, tiled=True)]
    ppermute x0 -> x1, starting transfers between devices: none -> 4.7 us  [per_device(): other = lax.ppermute(other, 'core', [(0, 1), (1, 0)])]
    pallas_call x13 -> x14, Pallas kernels: 5.32 us -> 5.51 us  [kernel_call(): pl.pallas_call(body, out_shape=out_shapes, in_specs=[pl.BlockSpec(memory_...]
  transfers between devices with their start and end apart: 0 -> 1, of which waited for: 0 -> 0; matrix products, arithmetic and copies ran while one was open for 0% -> 0% of each run, Pallas kernels for 0% -> 0%
where the time goes in v3:
time: 160 us; the launch traced here: 159 us
  blocking collectives  149 us (93%)
  Pallas kernels  5.51 us (3%)
  starting transfers between devices  4.7 us (3%)
    all_to_all x14, blocking collectives, exchange(): return lax.all_to_all(pieces, axes, 0, 0, tiled=True)  149 us
    pallas_call x14, Pallas kernels, kernel_call(): pl.pallas_call(body, out_shape=out_shapes, in_specs=[pl.BlockSpec(memory_...  5.51 us
    ppermute x1, starting transfers between devices, per_device(): other = lax.ppermute(other, 'core', [(0, 1), (1, 0)])  4.7 us
  transfers between devices with their start and end apart: 1, of which 0 were waited for; matrix products, arithmetic and copies ran while one was open for 0% of the time, Pallas kernels for 0%

profile of v3, /device:TPU:1, one launch (start us, length us, event | category | flops | bytes accessed | tf_op | source)
XLA Modules:
  0.0 159.1 jit_solution(8307917926451189206)
XLA Ops:
  0.0 0.0 copy-start.1
  0.0 0.0 copy-start
  0.0 2.0 %shard_map.91 = (f32[320,128]{1,0:T(8,128)S(1)}, f32[16,256]{1,0:T(8,128)S(1)}, f32[8,256]{1,0:T(8,128)S(1)}, f32[8,512]{1,0:T(8,128)S(1)}, f32[8,128]{1,0:T(8,128)S(1)}, /*index=5*/f32[8,128]{1,0:T(8,128)S(1)}) custom-call(bf16[16,256]{1,0:T(8,128)(2,1)} %tokens_hbm.1, bf16[256]{0:T(256)(128)(2,1)} %gain_hbm.1, bf16[256,2048]{1,0:T(8,128)(2,1)} %refs_3_.1, ...), custom_call_target="tpu_custom_call" | custom-call | tf_op jit(solution)/shard_map/pallas_call | solution.py:43
  2.1 14.8 %all_to_all.70 = f32[8,40,128]{2,1,0:T(8,128)S(1)} all-to-all(f32[8,40,128]{2,1,0:T(8,128)S(1)} %bitcast.14), channel_id=1, replica_groups=mesh['heads'=8,'y'=8,'x'=4,'core'=2] {'x','core'}, dimensions={0} | all-to-all | bytes 327680 | tf_op jit(solution)/shard_map/all_to_all | solution.py:316
  16.9 11.0 %all_to_all.71.refs_2_.parts_ref = f32[8,40,128]{2,1,0:T(8,128)S(1)} all-to-all(f32[8,40,128]{2,1,0:T(8,128)S(1)} %broadcast_in_dim.4), channel_id=1, replica_groups=mesh['heads'=8,'y'=8,'x'=4,'core'=2] {'y'}, dimensions={0} | all-to-all | bytes 327680 | tf_op jit(solution)/shard_map/all_to_all | solution.py:316
  28.0 0.0 copy-done.1
  28.0 0.0 copy-done
  28.0 0.0 copy-start.2
  28.0 0.1 shard_map.92
  28.1 4.7 %collective-permute-start = (f32[2,8,256,128]{3,2,1,0:T(8,128)S(1)}, f32[2,8,256,128]{3,2,1,0:T(8,128)S(1)}, u32[]{:S(2)}, u32[]{:S(2)}) collective-permute-start(f32[2,8,256,128]{3,2,1,0:T(8,128)S(1)} %shard_map.92), channel_id=1, source_target_pairs={{0,1},{1,0},{2,3},{3,2},{4,5},{5,4},{6,7},{7,6},{8,9},{9,8},{10,11... | collective-permute-start | bytes 6291464 | tf_op jit(solution)/shard_map/ppermute | solution.py:360
  32.8 0.1 shard_map.93
  32.9 6.9 %all_to_all.72.queries_ref = f32[4,32,128]{2,1,0:T(8,128)S(1)} all-to-all(f32[4,32,128]{2,1,0:T(8,128)S(1)} %get-tuple-element.22), channel_id=1, replica_groups=mesh['heads'=8,'y'=8,'x'=4,'core'=2] {'x'}, dimensions={0} | all-to-all | bytes 131072 | tf_op jit(solution)/shard_map/all_to_all | solution.py:316
  39.8 0.0 collective-permute-done.other_ref.refs_1_.refs_2_.refs_5_
  39.8 0.0 copy-done.2
  39.8 0.6 shard_map.94
  40.4 6.9 %all_to_all.73.refs_0_ = f32[4,40,128]{2,1,0:T(8,128)S(1)} all-to-all(f32[4,40,128]{2,1,0:T(8,128)S(1)} %shard_map.94), channel_id=1, replica_groups=mesh['heads'=8,'y'=8,'x'=4,'core'=2] {'x'}, dimensions={0} | all-to-all | bytes 163840 | tf_op jit(solution)/shard_map/all_to_all | solution.py:316
  47.3 0.0 copy-start.4
  47.3 0.1 shard_map.95
  47.4 10.9 %all_to_all.74.refs_0_ = f32[8,40,128]{2,1,0:T(8,128)S(1)} all-to-all(f32[8,40,128]{2,1,0:T(8,128)S(1)} %shard_map.95), channel_id=1, replica_groups=mesh['heads'=8,'y'=8,'x'=4,'core'=2] {'y'}, dimensions={0} | all-to-all | bytes 327680 | tf_op jit(solution)/shard_map/all_to_all | solution.py:316
  58.3 0.1 shard_map.96
  58.5 0.0 copy-start.6
  58.5 0.0 copy-start.7
  58.5 11.1 %all_to_all.75 = f32[8,32,128]{2,1,0:T(8,128)S(1)} all-to-all(f32[8,32,128]{2,1,0:T(8,128)S(1)} %shard_map.96), channel_id=1, replica_groups=mesh['heads'=8,'y'=8,'x'=4,'core'=2] {'x','core'}, dimensions={0} | all-to-all | bytes 262144 | tf_op jit(solution)/shard_map/all_to_all | solution.py:316
  69.6 0.0 copy-done.4
  69.6 0.3 shard_map.97
  69.9 17.7 %all_to_all.76.refs_0_ = f32[8,16,256]{2,1,0:T(8,128)S(1)} all-to-all(f32[8,16,256]{2,1,0:T(8,128)S(1)} %shard_map.97), channel_id=1, replica_groups=mesh['heads'=8,'y'=8,'x'=4,'core'=2] {'heads'}, dimensions={0} | all-to-all | bytes 262144 | tf_op jit(solution)/shard_map/all_to_all | solution.py:316
  87.6 0.0 copy-done.6
  87.6 0.0 copy-done.7
  87.6 0.3 shard_map.98
  87.9 10.3 %all_to_all.77 = f32[8,40,128]{2,1,0:T(8,128)S(1)} all-to-all(f32[8,40,128]{2,1,0:T(8,128)S(1)} %bitcast.15), channel_id=1, replica_groups=mesh['heads'=8,'y'=8,'x'=4,'core'=2] {'x','core'}, dimensions={0} | all-to-all | bytes 327680 | tf_op jit(solution)/shard_map/all_to_all | solution.py:316
  98.2 0.0 copy-start.3
  98.3 10.7 %all_to_all.78.refs_0_ = f32[8,40,128]{2,1,0:T(8,128)S(1)} all-to-all(f32[8,40,128]{2,1,0:T(8,128)S(1)} %broadcast_in_dim.5), channel_id=1, replica_groups=mesh['heads'=8,'y'=8,'x'=4,'core'=2] {'y'}, dimensions={0} | all-to-all | bytes 327680 | tf_op jit(solution)/shard_map/all_to_all | solution.py:316
  109.0 0.1 shard_map.99
  109.1 6.8 %all_to_all.79.queries_ref = f32[4,32,128]{2,1,0:T(8,128)S(1)} all-to-all(f32[4,32,128]{2,1,0:T(8,128)S(1)} %get-tuple-element.30), channel_id=1, replica_groups=mesh['heads'=8,'y'=8,'x'=4,'core'=2] {'x'}, dimensions={0} | all-to-all | bytes 131072 | tf_op jit(solution)/shard_map/all_to_all | solution.py:316
  115.9 0.0 copy-done.3
  115.9 0.0 copy-start.5
  115.9 0.6 shard_map.100
  116.5 6.9 %all_to_all.80.parts_ref = f32[4,40,128]{2,1,0:T(8,128)S(1)} all-to-all(f32[4,40,128]{2,1,0:T(8,128)S(1)} %shard_map.100), channel_id=1, replica_groups=mesh['heads'=8,'y'=8,'x'=4,'core'=2] {'x'}, dimensions={0} | all-to-all | bytes 163840 | tf_op jit(solution)/shard_map/all_to_all | solution.py:316
  123.5 0.1 shard_map.101
  123.6 10.7 %all_to_all.81.parts_ref = f32[8,40,128]{2,1,0:T(8,128)S(1)} all-to-all(f32[8,40,128]{2,1,0:T(8,128)S(1)} %shard_map.101), channel_id=1, replica_groups=mesh['heads'=8,'y'=8,'x'=4,'core'=2] {'y'}, dimensions={0} | all-to-all | bytes 327680 | tf_op jit(solution)/shard_map/all_to_all | solution.py:316
  134.3 0.1 shard_map.102
  134.4 13.6 %all_to_all.82 = f32[8,32,128]{2,1,0:T(8,128)S(1)} all-to-all(f32[8,32,128]{2,1,0:T(8,128)S(1)} %shard_map.102), channel_id=1, replica_groups=mesh['heads'=8,'y'=8,'x'=4,'core'=2] {'x','core'}, dimensions={0} | all-to-all | bytes 262144 | tf_op jit(solution)/shard_map/all_to_all | solution.py:316
  148.0 0.0 copy-done.5
  148.0 0.3 shard_map.103
  148.3 10.1 %all_to_all.83.sums_ref = f32[8,16,256]{2,1,0:T(8,128)S(1)} all-to-all(f32[8,16,256]{2,1,0:T(8,128)S(1)} %shard_map.103), channel_id=1, replica_groups=mesh['heads'=8,'y'=8,'x'=4,'core'=2] {'heads'}, dimensions={0} | all-to-all | bytes 262144 | tf_op jit(solution)/shard_map/all_to_all | solution.py:316
  158.4 0.6 shard_map.104
  (4 shorter events, 0.1 us)
Async XLA Ops:
  0.0 28.0 %copy-start.1 = (bf16[1,16,256,128]{3,2,1,0:T(8,128)(2,1)S(1)}, bf16[1,16,256,128]{3,2,1,0:T(8,128)(2,1)}, u32[]{:S(2)}) copy-start(bf16[1,16,256,128]{3,2,1,0:T(8,128)(2,1)} %param.15) | copy-start | bytes 3145732
  0.0 28.0 %copy-start = (bf16[1,16,256,128]{3,2,1,0:T(8,128)(2,1)S(1)}, bf16[1,16,256,128]{3,2,1,0:T(8,128)(2,1)}, u32[]{:S(2)}) copy-start(bf16[1,16,256,128]{3,2,1,0:T(8,128)(2,1)} %param.14) | copy-start | bytes 3145732
  28.0 11.8 %copy-start.2 = (bf16[1,16,256,128]{3,2,1,0:T(8,128)(2,1)S(1)}, bf16[1,16,256,128]{3,2,1,0:T(8,128)(2,1)}, u32[]{:S(2)}) copy-start(bf16[1,16,256,128]{3,2,1,0:T(8,128)(2,1)} %param.15) | copy-start | bytes 3145732
  28.1 11.6 %collective-permute-start = (f32[2,8,256,128]{3,2,1,0:T(8,128)S(1)}, f32[2,8,256,128]{3,2,1,0:T(8,128)S(1)}, u32[]{:S(2)}, u32[]{:S(2)}) collective-permute-start(f32[2,8,256,128]{3,2,1,0:T(8,128)S(1)} %shard_map.92), channel_id=1, source_target_pairs={{0,1},{1,0},{2,3},{3,2},{4,5},{5,4},{6,7},{7,6},{8,9},{9,8},{10,11... | collective-permute-start | bytes 6291464 | tf_op jit(solution)/shard_map/ppermute | solution.py:360
  47.3 22.3 %copy-start.4 = (bf16[2048,256]{1,0:T(8,128)(2,1)S(1)}, bf16[2048,256]{1,0:T(8,128)(2,1)}, u32[]{:S(2)}) copy-start(bf16[2048,256]{1,0:T(8,128)(2,1)} %wout_ref.1) | copy-start | bytes 3145732
  58.5 29.1 %copy-start.6 = (bf16[256,2048]{1,0:T(8,128)(2,1)S(1)}, bf16[256,2048]{1,0:T(8,128)(2,1)}, u32[]{:S(2)}) copy-start(bf16[256,2048]{1,0:T(8,128)(2,1)} %refs_3_.1) | copy-start | bytes 3145732
  58.5 29.1 %copy-start.7 = (bf16[256,256]{1,0:T(8,128)(2,1)S(1)}, bf16[256,256]{1,0:T(8,128)(2,1)}, u32[]{:S(2)}) copy-start(bf16[256,256]{1,0:T(8,128)(2,1)} %refs_4_.1) | copy-start | bytes 393220
  98.2 17.7 %copy-start.3 = (bf16[1,16,256,128]{3,2,1,0:T(8,128)(2,1)S(1)}, bf16[1,16,256,128]{3,2,1,0:T(8,128)(2,1)}, u32[]{:S(2)}) copy-start(bf16[1,16,256,128]{3,2,1,0:T(8,128)(2,1)} %param.15) | copy-start | bytes 3145732
  115.9 32.1 %copy-start.5 = (bf16[2048,256]{1,0:T(8,128)(2,1)S(1)}, bf16[2048,256]{1,0:T(8,128)(2,1)}, u32[]{:S(2)}) copy-start(bf16[2048,256]{1,0:T(8,128)(2,1)} %wout_ref.1) | copy-start | bytes 3145732

commit v4 on v3

--- a/solution.py
+++ b/solution.py
@@ -24,7 +24,8 @@
 OWN = ROWS // GROUP
 PIECE = 40
 BATCH = 2
-CHUNKS = 4
+CHUNKS = 2
+DENSE = 33
 SCALE = 1.0 / math.sqrt(DIM)
 F32 = jnp.float32
 BF16 = jnp.bfloat16
@@ -99,7 +100,7 @@
     columns = [pl.ds(c * chunk, chunk) for c in range(CHUNKS)]
     pairs += [(wq_hbm.at[:, c], wq_ref.at[:, c]) for c in columns]
     copies = [pltpu.make_async_copy(a, b, sems.at[i]) for i, (a, b) in enumerate(pairs)]
-    for copy in copies:
+    for copy in copies[5:] + copies[:5]:
         copy.start()
     inner = lax.axis_index("x") * 2 + lax.axis_index("core")
     core = lax.axis_index("core")
@@ -198,9 +199,9 @@
     return jnp.sum(jnp.where(diagonal(), line, 0.0), axis=1, keepdims=True)
 
 
-def stats_block(top, total):
-    line = lax.broadcasted_iota(jnp.int32, (PIECE - 2 * HEADS, DIM), 0)
-    return jnp.where(line == 0, top, jnp.where(line == 1, total, 0.0))
+def joined(top, total):
+    lane = lax.broadcasted_iota(jnp.int32, (1, DIM), 1)
+    return jnp.where(lane < 2 * HEADS, top, jnp.where(lane < 4 * HEADS, pltpu.roll(total, 2 * HEADS, 1), 0.0))
 
 
 def swap_kernel(keys_ref, values_ref, other_ref):
@@ -236,7 +237,8 @@
         for b in range(0, BATCH, OWN):
             top = tops[b : b + OWN].reshape(OWN * HEADS, 1)
             total = totals[b : b + OWN].reshape(OWN * HEADS, 1)
-            pieces_ref[(c + b) // OWN, 2 * HEADS :, :] = stats_block(to_lanes(top), to_lanes(total))
+            stats = joined(to_lanes(top), to_lanes(total))
+            pieces_ref[(c + b) // OWN, 2 * HEADS :, :] = jnp.broadcast_to(stats, (PIECE - 2 * HEADS, DIM))
     for i in range(ROWS // 2):
         x, heads = place(i)
         own, other = (work_ref[i, :, half].astype(BF16) for half in halves)
@@ -245,25 +247,26 @@
         ) + jnp.dot(other, other_ref[1, i].astype(BF16), preferred_element_type=F32)
 
 
-def merge(parts_ref):
-    tops = [parts_ref[s, 2 * HEADS : 2 * HEADS + 1, :] for s in range(parts_ref.shape[0])]
-    top = functools.reduce(jnp.maximum, tops)
-    total, weighted = None, None
-    for s in range(parts_ref.shape[0]):
-        factor = jnp.exp(tops[s] - top)
-        here = factor * parts_ref[s, 2 * HEADS + 1 : 2 * HEADS + 2, :]
-        part = to_column(factor) * parts_ref[s, : 2 * HEADS, :]
+def merge(weighted, stats):
+    top = functools.reduce(jnp.maximum, stats)
+    total, whole = None, None
+    for part, stat in zip(weighted, stats):
+        factor = jnp.exp(stat - top)
+        here = factor * pltpu.roll(stat, DIM - 2 * HEADS, 1)
+        part = to_column(factor) * part
         total = here if total is None else total + here
-        weighted = part if weighted is None else weighted + part
-    return top, total, weighted
+        whole = part if whole is None else whole + part
+    return top, total, whole
 
 
 def merge_kernel(parts_ref, pieces_ref):
-    top, total, weighted = merge(parts_ref)
-    stats = stats_block(top, total)
+    top, total, weighted = merge(*zip(*[
+        (parts_ref[s, : 2 * HEADS, :], parts_ref[s, 2 * HEADS : 2 * HEADS + 1, :]) for s in range(parts_ref.shape[0])
+    ]))
+    stats = joined(top, total)
     for d in range(GROUP):
-        pieces_ref[d, : 2 * HEADS, :] = weighted
-        pieces_ref[d, 2 * HEADS :, :] = stats
+        pieces_ref[d * DENSE : d * DENSE + 2 * HEADS, :] = weighted
+        pieces_ref[d * DENSE + 2 * HEADS : (d + 1) * DENSE, :] = stats
 
 
 def finish_kernel(parts_ref, *refs):
@@ -277,7 +280,10 @@
             [jnp.broadcast_to(rounded(ref[line + r : line + r + 1, :]), (HEADS, DIM)) for r in range(OWN)], axis=0
         )
 
-    top, total, weighted = merge(parts_ref)
+    top, total, weighted = merge(*zip(*[
+        (parts_ref[s * DENSE : s * DENSE + 2 * HEADS, :], parts_ref[s * DENSE + 2 * HEADS : (s + 1) * DENSE, :])
+        for s in range(GROUP)
+    ]))
     top, total = to_column(top), to_column(total)
     queries = rounded(own_refs[-1][: 2 * HEADS, :])
     scores = [jnp.sum(queries * spread(ref, 2 * HEADS), axis=1, keepdims=True) * SCALE for ref in own_refs]
@@ -321,7 +327,6 @@
     width = tokens.shape[1]
     keys, values = key_cache[0], value_cache[0]
     flat = shape(GROUP * PIECE, DIM)
-    cube = shape(GROUP, PIECE, DIM)
     half = pltpu.VMEM((ROWS, width // 2), F32)
     work = pltpu.VMEM((ROWS // 2, HEADS, 2 * seq_here), F32)
     line = shape(8, DIM)
@@ -366,7 +371,8 @@
         )
         parts = exchange(pieces, ("x",))
         kept = () if step else (other,)
-        parts = exchange(kernel_call(merge_kernel, cube, parts, after=kept), ("y",))
+        pieces = kernel_call(merge_kernel, shape(GROUP * DENSE, DIM), parts, after=kept)
+        parts = exchange(pieces.reshape(GROUP, 1, DENSE * DIM), ("y",)).reshape(GROUP * DENSE, DIM)
         pieces = kernel_call(finish_kernel, shape(GROUP, 2 * HEADS, DIM), parts, *own, after=kept)
         attended = exchange(pieces, INNER).reshape(GROUP * 2 * HEADS, DIM)
         sums = exchange(kernel_call(out_kernel, shape(GROUP, ROWS, width), attended, w_out, after=kept), ("heads",))

time: 160 us -> 159 us (level)
  no operation moved by 1% of the time
where the time goes in v4:
time: 159 us; the launch traced here: 158 us
  blocking collectives  148 us (93%)
  Pallas kernels  5.57 us (4%)
  starting transfers between devices  4.7 us (3%)
    all_to_all x14, blocking collectives, exchange(): return lax.all_to_all(pieces, axes, 0, 0, tiled=True)  148 us
    pallas_call x14, Pallas kernels, kernel_call(): pl.pallas_call(body, out_shape=out_shapes, in_specs=[pl.BlockSpec(memory_...  5.57 us
    ppermute x1, starting transfers between devices, per_device(): other = lax.ppermute(other, 'core', [(0, 1), (1, 0)])  4.7 us
  transfers between devices with their start and end apart: 1, of which 0 were waited for; matrix products, arithmetic and copies ran while one was open for 0% of the time, Pallas kernels for 0%

profile of v4, /device:TPU:1, one launch (start us, length us, event | category | flops | bytes accessed | tf_op | source)
XLA Modules:
  0.0 158.5 jit_solution(6915264746427836687)
XLA Ops:
  0.0 0.0 copy-start.1
  0.0 0.0 copy-start
  0.0 1.8 %shard_map.91 = (f32[320,128]{1,0:T(8,128)S(1)}, f32[16,256]{1,0:T(8,128)S(1)}, f32[8,256]{1,0:T(8,128)S(1)}, f32[8,512]{1,0:T(8,128)S(1)}, f32[8,128]{1,0:T(8,128)S(1)}, /*index=5*/f32[8,128]{1,0:T(8,128)S(1)}) custom-call(bf16[16,256]{1,0:T(8,128)(2,1)} %tokens_hbm.1, bf16[256]{0:T(256)(128)(2,1)} %gain_hbm.1, bf16[256,2048]{1,0:T(8,128)(2,1)} %refs_3_.1, ...), custom_call_target="tpu_custom_call" | custom-call | tf_op jit(solution)/shard_map/pallas_call | solution.py:44
  1.8 14.8 %all_to_all.70 = f32[8,40,128]{2,1,0:T(8,128)S(1)} all-to-all(f32[8,40,128]{2,1,0:T(8,128)S(1)} %bitcast.22), channel_id=1, replica_groups=mesh['heads'=8,'y'=8,'x'=4,'core'=2] {'x','core'}, dimensions={0} | all-to-all | bytes 327680 | tf_op jit(solution)/shard_map/all_to_all | solution.py:322
  16.7 11.0 %all_to_all.71.refs_2_.parts_ref = f32[8,40,128]{2,1,0:T(8,128)S(1)} all-to-all(f32[8,40,128]{2,1,0:T(8,128)S(1)} %broadcast_in_dim.4), channel_id=1, replica_groups=mesh['heads'=8,'y'=8,'x'=4,'core'=2] {'y'}, dimensions={0} | all-to-all | bytes 327680 | tf_op jit(solution)/shard_map/all_to_all | solution.py:322
  27.7 0.0 copy-done.1
  27.7 0.0 copy-done
  27.7 0.0 copy-start.2
  27.7 0.1 shard_map.92
  27.9 4.7 %collective-permute-start = (f32[2,8,256,128]{3,2,1,0:T(8,128)S(1)}, f32[2,8,256,128]{3,2,1,0:T(8,128)S(1)}, u32[]{:S(2)}, u32[]{:S(2)}) collective-permute-start(f32[2,8,256,128]{3,2,1,0:T(8,128)S(1)} %shard_map.92), channel_id=1, source_target_pairs={{0,1},{1,0},{2,3},{3,2},{4,5},{5,4},{6,7},{7,6},{8,9},{9,8},{10,11... | collective-permute-start | bytes 6291464 | tf_op jit(solution)/shard_map/ppermute | solution.py:365
  32.6 0.1 shard_map.93
  32.6 6.9 %all_to_all.72.queries_ref = f32[4,32,128]{2,1,0:T(8,128)S(1)} all-to-all(f32[4,32,128]{2,1,0:T(8,128)S(1)} %get-tuple-element.22), channel_id=1, replica_groups=mesh['heads'=8,'y'=8,'x'=4,'core'=2] {'x'}, dimensions={0} | all-to-all | bytes 131072 | tf_op jit(solution)/shard_map/all_to_all | solution.py:322
  39.5 0.0 collective-permute-done.other_ref.refs_1_.refs_2_.refs_5_
  39.5 0.0 copy-done.2
  39.5 0.6 shard_map.94
  40.2 6.9 %all_to_all.73.refs_0_ = f32[4,40,128]{2,1,0:T(8,128)S(1)} all-to-all(f32[4,40,128]{2,1,0:T(8,128)S(1)} %shard_map.94), channel_id=1, replica_groups=mesh['heads'=8,'y'=8,'x'=4,'core'=2] {'x'}, dimensions={0} | all-to-all | bytes 163840 | tf_op jit(solution)/shard_map/all_to_all | solution.py:322
  47.1 0.0 copy-start.4
  47.1 0.1 shard_map.95
  47.2 10.6 %all_to_all.74 = f32[8,1,4224]{2,1,0:T(1,128)S(1)} all-to-all(f32[8,1,4224]{2,1,0:T(1,128)S(1)} %bitcast.17), channel_id=1, replica_groups=mesh['heads'=8,'y'=8,'x'=4,'core'=2] {'y'}, dimensions={0} | all-to-all | bytes 270336 | tf_op jit(solution)/shard_map/all_to_all | solution.py:322
  57.8 0.2 shard_map.96
  58.1 0.0 copy-start.6
  58.1 0.0 copy-start.7
  58.1 11.1 %all_to_all.75 = f32[8,32,128]{2,1,0:T(8,128)S(1)} all-to-all(f32[8,32,128]{2,1,0:T(8,128)S(1)} %shard_map.96), channel_id=1, replica_groups=mesh['heads'=8,'y'=8,'x'=4,'core'=2] {'x','core'}, dimensions={0} | all-to-all | bytes 262144 | tf_op jit(solution)/shard_map/all_to_all | solution.py:322
  69.2 0.0 copy-done.4
  69.2 0.3 shard_map.97
  69.5 17.7 %all_to_all.76.refs_0_ = f32[8,16,256]{2,1,0:T(8,128)S(1)} all-to-all(f32[8,16,256]{2,1,0:T(8,128)S(1)} %shard_map.97), channel_id=1, replica_groups=mesh['heads'=8,'y'=8,'x'=4,'core'=2] {'heads'}, dimensions={0} | all-to-all | bytes 262144 | tf_op jit(solution)/shard_map/all_to_all | solution.py:322
  87.2 0.0 copy-done.6
  87.2 0.0 copy-done.7
  87.2 0.3 shard_map.98
  87.4 10.3 %all_to_all.77 = f32[8,40,128]{2,1,0:T(8,128)S(1)} all-to-all(f32[8,40,128]{2,1,0:T(8,128)S(1)} %bitcast.23), channel_id=1, replica_groups=mesh['heads'=8,'y'=8,'x'=4,'core'=2] {'x','core'}, dimensions={0} | all-to-all | bytes 327680 | tf_op jit(solution)/shard_map/all_to_all | solution.py:322
  97.8 0.0 copy-start.3
  97.8 10.7 %all_to_all.78.refs_0_ = f32[8,40,128]{2,1,0:T(8,128)S(1)} all-to-all(f32[8,40,128]{2,1,0:T(8,128)S(1)} %broadcast_in_dim.5), channel_id=1, replica_groups=mesh['heads'=8,'y'=8,'x'=4,'core'=2] {'y'}, dimensions={0} | all-to-all | bytes 327680 | tf_op jit(solution)/shard_map/all_to_all | solution.py:322
  108.6 0.1 shard_map.99
  108.7 6.8 %all_to_all.79.queries_ref = f32[4,32,128]{2,1,0:T(8,128)S(1)} all-to-all(f32[4,32,128]{2,1,0:T(8,128)S(1)} %get-tuple-element.30), channel_id=1, replica_groups=mesh['heads'=8,'y'=8,'x'=4,'core'=2] {'x'}, dimensions={0} | all-to-all | bytes 131072 | tf_op jit(solution)/shard_map/all_to_all | solution.py:322
  115.5 0.0 copy-done.3
  115.5 0.0 copy-start.5
  115.5 0.7 shard_map.100
  116.2 6.9 %all_to_all.80.parts_ref = f32[4,40,128]{2,1,0:T(8,128)S(1)} all-to-all(f32[4,40,128]{2,1,0:T(8,128)S(1)} %shard_map.100), channel_id=1, replica_groups=mesh['heads'=8,'y'=8,'x'=4,'core'=2] {'x'}, dimensions={0} | all-to-all | bytes 163840 | tf_op jit(solution)/shard_map/all_to_all | solution.py:322
  123.1 0.1 shard_map.101
  123.2 10.4 %all_to_all.81 = f32[8,1,4224]{2,1,0:T(1,128)S(1)} all-to-all(f32[8,1,4224]{2,1,0:T(1,128)S(1)} %bitcast.19), channel_id=1, replica_groups=mesh['heads'=8,'y'=8,'x'=4,'core'=2] {'y'}, dimensions={0} | all-to-all | bytes 270336 | tf_op jit(solution)/shard_map/all_to_all | solution.py:322
  133.6 0.2 shard_map.102
  133.8 13.6 %all_to_all.82 = f32[8,32,128]{2,1,0:T(8,128)S(1)} all-to-all(f32[8,32,128]{2,1,0:T(8,128)S(1)} %shard_map.102), channel_id=1, replica_groups=mesh['heads'=8,'y'=8,'x'=4,'core'=2] {'x','core'}, dimensions={0} | all-to-all | bytes 262144 | tf_op jit(solution)/shard_map/all_to_all | solution.py:322
  147.4 0.0 copy-done.5
  147.4 0.3 shard_map.103
  147.7 10.1 %all_to_all.83.sums_ref = f32[8,16,256]{2,1,0:T(8,128)S(1)} all-to-all(f32[8,16,256]{2,1,0:T(8,128)S(1)} %shard_map.103), channel_id=1, replica_groups=mesh['heads'=8,'y'=8,'x'=4,'core'=2] {'heads'}, dimensions={0} | all-to-all | bytes 262144 | tf_op jit(solution)/shard_map/all_to_all | solution.py:322
  157.8 0.6 shard_map.104
  (4 shorter events, 0.1 us)
Async XLA Ops:
  0.0 27.7 %copy-start.1 = (bf16[1,16,256,128]{3,2,1,0:T(8,128)(2,1)S(1)}, bf16[1,16,256,128]{3,2,1,0:T(8,128)(2,1)}, u32[]{:S(2)}) copy-start(bf16[1,16,256,128]{3,2,1,0:T(8,128)(2,1)} %param.15) | copy-start | bytes 3145732
  0.0 27.7 %copy-start = (bf16[1,16,256,128]{3,2,1,0:T(8,128)(2,1)S(1)}, bf16[1,16,256,128]{3,2,1,0:T(8,128)(2,1)}, u32[]{:S(2)}) copy-start(bf16[1,16,256,128]{3,2,1,0:T(8,128)(2,1)} %param.14) | copy-start | bytes 3145732
  27.7 11.8 %copy-start.2 = (bf16[1,16,256,128]{3,2,1,0:T(8,128)(2,1)S(1)}, bf16[1,16,256,128]{3,2,1,0:T(8,128)(2,1)}, u32[]{:S(2)}) copy-start(bf16[1,16,256,128]{3,2,1,0:T(8,128)(2,1)} %param.15) | copy-start | bytes 3145732
  27.9 11.6 %collective-permute-start = (f32[2,8,256,128]{3,2,1,0:T(8,128)S(1)}, f32[2,8,256,128]{3,2,1,0:T(8,128)S(1)}, u32[]{:S(2)}, u32[]{:S(2)}) collective-permute-start(f32[2,8,256,128]{3,2,1,0:T(8,128)S(1)} %shard_map.92), channel_id=1, source_target_pairs={{0,1},{1,0},{2,3},{3,2},{4,5},{5,4},{6,7},{7,6},{8,9},{9,8},{10,11... | collective-permute-start | bytes 6291464 | tf_op jit(solution)/shard_map/ppermute | solution.py:365
  47.1 22.1 %copy-start.4 = (bf16[2048,256]{1,0:T(8,128)(2,1)S(1)}, bf16[2048,256]{1,0:T(8,128)(2,1)}, u32[]{:S(2)}) copy-start(bf16[2048,256]{1,0:T(8,128)(2,1)} %wout_ref.1) | copy-start | bytes 3145732
  58.1 29.1 %copy-start.6 = (bf16[256,2048]{1,0:T(8,128)(2,1)S(1)}, bf16[256,2048]{1,0:T(8,128)(2,1)}, u32[]{:S(2)}) copy-start(bf16[256,2048]{1,0:T(8,128)(2,1)} %refs_3_.1) | copy-start | bytes 3145732
  58.1 29.1 %copy-start.7 = (bf16[256,256]{1,0:T(8,128)(2,1)S(1)}, bf16[256,256]{1,0:T(8,128)(2,1)}, u32[]{:S(2)}) copy-start(bf16[256,256]{1,0:T(8,128)(2,1)} %refs_4_.1) | copy-start | bytes 393220
  97.8 17.7 %copy-start.3 = (bf16[1,16,256,128]{3,2,1,0:T(8,128)(2,1)S(1)}, bf16[1,16,256,128]{3,2,1,0:T(8,128)(2,1)}, u32[]{:S(2)}) copy-start(bf16[1,16,256,128]{3,2,1,0:T(8,128)(2,1)} %param.15) | copy-start | bytes 3145732
  115.5 31.9 %copy-start.5 = (bf16[2048,256]{1,0:T(8,128)(2,1)S(1)}, bf16[2048,256]{1,0:T(8,128)(2,1)}, u32[]{:S(2)}) copy-start(bf16[2048,256]{1,0:T(8,128)(2,1)} %wout_ref.1) | copy-start | bytes 3145732

commit v5 on v4

--- a/solution.py
+++ b/solution.py
@@ -26,6 +26,8 @@
 BATCH = 2
 CHUNKS = 2
 DENSE = 33
+SHARE = 5
+QUARTER = HEADS // 4
 SCALE = 1.0 / math.sqrt(DIM)
 F32 = jnp.float32
 BF16 = jnp.bfloat16
@@ -59,27 +61,34 @@
     return i // OWN * (2 * OWN) + core * OWN + i % OWN
 
 
-def project(wide, gain_ref, wq_ref, wkv_ref, pieces_ref, waits=None):
+def project(wide, gain_ref, wq_ref, wkv_ref, pieces_ref, waits=None, shares=False):
     gained = (wide * gain_ref[0:1, :]).astype(BF16)
 
-    def put(row, block):
+    def put(head, block):
         for r in range(OWN):
-            pieces_ref[pl.ds(row(r), GROUP, stride=PIECE), :] = block[r * GROUP : (r + 1) * GROUP]
+            if not shares:
+                start = r * HEADS + head if head < HEADS else 2 * HEADS + (head - HEADS) * OWN + r
+            elif head < HEADS:
+                start = (r * 4 + head // QUARTER) * GROUP * SHARE + head % QUARTER
+            else:
+                start = (r * 4 + head - HEADS) * GROUP * SHARE + SHARE - 1
+            stride = SHARE if shares else PIECE
+            pieces_ref[pl.ds(start, GROUP, stride=stride), :] = block[r * GROUP : (r + 1) * GROUP]
 
     for j in range(HEADS // 2):
         if waits:
             waits[j]()
         both = jnp.dot(gained, wq_ref[:, 2 * j * DIM : 2 * (j + 1) * DIM], preferred_element_type=F32)
         for k in range(2):
-            put(lambda r: r * HEADS + 2 * j + k, both[:, k * DIM : (k + 1) * DIM])
+            put(2 * j + k, both[:, k * DIM : (k + 1) * DIM])
     if waits:
         waits[-1]()
     both = jnp.dot(gained, wkv_ref[...], preferred_element_type=F32)
-    put(lambda r: 2 * HEADS + r, both[:, :DIM])
-    put(lambda r: 2 * HEADS + OWN + r, both[:, DIM:])
+    put(HEADS + 0, both[:, :DIM])
+    put(HEADS + 1, both[:, DIM:])
     squares = jnp.broadcast_to(jnp.sum(wide * wide, axis=1, keepdims=True), (ROWS, DIM))
-    put(lambda r: 2 * HEADS + 2 * OWN + r, squares)
-    put(lambda r: 2 * HEADS + 3 * OWN + r, jnp.zeros((ROWS, DIM), F32))
+    put(HEADS + 2, squares)
+    put(HEADS + 3, jnp.zeros((ROWS, DIM), F32))
 
 
 def first_kernel(
@@ -118,11 +127,14 @@
     line = lax.broadcasted_iota(jnp.int32, (8, DIM), 0)
     index = jnp.where(lane < DIM // 2, lane, lane - DIM // 2).astype(F32)
     freqs = jnp.exp(index * (-2.0 * math.log(ROPE_BASE) / DIM))
-    place = jnp.where(line % 2 == 1, positions_ref[inner * OWN + 1], positions_ref[inner * OWN])
+    both = (positions_ref[inner * OWN], positions_ref[inner * OWN + 1])
+    one = jnp.where(lax.axis_index("y") >= 4, both[1], both[0])
     for step, ref in enumerate(table_refs):
+        place = jnp.where(line % 2 == 1, both[1], both[0]) if step == 0 else jnp.broadcast_to(one, line.shape)
         angles = (place + step).astype(F32) * freqs
         sine = jnp.sin(angles)
-        ref[...] = jnp.where(line < OWN, jnp.cos(angles), jnp.where(lane < DIM // 2, -sine, sine))
+        cosines = line < OWN if step == 0 else line == 0
+        ref[...] = jnp.where(cosines, jnp.cos(angles), jnp.where(lane < DIM // 2, -sine, sine))
     copies[2].wait()
     copies[3].wait()
     width = tokens_ref.shape[1] // 2
@@ -147,7 +159,7 @@
         output = output + sums_ref[s]
     output_ref[...] = output
     wide = (last_ref[...] + output).astype(BF16).astype(F32)
-    project(wide, gain_ref, wq_ref, wkv_ref, pieces_ref)
+    project(wide, gain_ref, wq_ref, wkv_ref, pieces_ref, shares=True)
 
 
 def last_kernel(sums_ref, first_ref, result_ref):
@@ -181,9 +193,27 @@
     sines = jnp.where(line < OWN, jnp.where(odd, sine[1], sine[0]), 0.0)
     blocks.append(scaled * cosines + pltpu.roll(scaled, DIM // 2, 1) * sines)
     piece = jnp.concatenate(blocks, axis=0)
-    own_ref[...] = piece
+    own_ref[0] = piece
     for d in range(pieces_ref.shape[0]):
         pieces_ref[d] = piece[: 2 * HEADS]
+
+
+def turn_shares_kernel(parts_ref, table_ref, pieces_ref):
+    step = GROUP * SHARE
+    sums = []
+    for t in range(SHARE):
+        total = parts_ref[pl.ds(t, GROUP, stride=SHARE), :]
+        for k in range(step, parts_ref.shape[0], step):
+            total = total + parts_ref[pl.ds(k + t, GROUP, stride=SHARE), :]
+        sums.append(jnp.sum(total, axis=0, keepdims=True))
+    whole = jnp.concatenate(sums, axis=0)
+    turned = whole * table_ref[0:1, :] + pltpu.roll(whole, DIM // 2, 1) * table_ref[1:2, :]
+    line = lax.broadcasted_iota(jnp.int32, whole.shape, 0)
+    quarter = jnp.broadcast_to(lax.rem(lax.axis_index("y"), 4), whole.shape)
+    piece = jnp.where((line < SHARE - 1) | (quarter == 0), turned, whole)
+    copies = jnp.concatenate([piece] * GROUP, axis=0)
+    for k in range(0, pieces_ref.shape[0], step):
+        pieces_ref[k : k + step, :] = copies
 
 
 def diagonal():
@@ -212,7 +242,8 @@
         other_ref[1, i] = values_ref[b].astype(F32)
 
 
-def attend_kernel(queries_ref, keys_ref, values_ref, other_ref, seen_ref, pieces_ref, work_ref):
+def attend_kernel(queries_ref, keys_ref, values_ref, other_ref, seen_ref, pieces_ref, *refs):
+    own_ref, work_ref = (None, *refs)[-2:]
     core = lax.axis_index("core")
     seq_here = keys_ref.shape[1]
     halves = (slice(0, seq_here), slice(seq_here, 2 * seq_here))
@@ -222,7 +253,18 @@
 
     for i in range(ROWS // 2):
         x, heads = place(i)
-        queries = queries_ref[x, heads, :].astype(BF16)
+        if own_ref is None:
+            scaled = queries_ref[x, heads, :]
+        else:
+            starts = [((i % OWN * 4 + quarter) * (GROUP // 2) + x) * SHARE for quarter in range(4)]
+            ends = [queries_ref[start + SHARE - 1 : start + SHARE, :] for start in starts]
+            inverse = lax.rsqrt(ends[2] / D + EPSILON)
+            scaled = jnp.concatenate([queries_ref[start : start + QUARTER, :] for start in starts], axis=0) * inverse
+            own_ref[x, heads, :] = scaled
+            for k in range(2):
+                line = 2 * HEADS + k * OWN + i % OWN
+                own_ref[x, line : line + 1, :] = ends[k] * inverse
+        queries = scaled.astype(BF16)
         for half, keys in zip(halves, (keys_ref[core_row(i, core)], other_ref[0, i].astype(BF16))):
             work_ref[i, :, half] = lax.dot_general(
                 queries, keys, (((1,), (1,)), ((), ())), preferred_element_type=F32
@@ -271,13 +313,14 @@
 
 def finish_kernel(parts_ref, *refs):
     own_refs, pieces_ref = refs[:-1], refs[-1]
+    x = lax.axis_index("x")
 
     def rounded(value):
         return value.astype(BF16).astype(F32)
 
     def spread(ref, line):
         return jnp.concatenate(
-            [jnp.broadcast_to(rounded(ref[line + r : line + r + 1, :]), (HEADS, DIM)) for r in range(OWN)], axis=0
+            [jnp.broadcast_to(rounded(ref[x if ref.shape[0] > 1 else 0, line + r : line + r + 1, :]), (HEADS, DIM)) for r in range(OWN)], axis=0
         )
 
     top, total, weighted = merge(*zip(*[
@@ -285,7 +328,7 @@
         for s in range(GROUP)
     ]))
     top, total = to_column(top), to_column(total)
-    queries = rounded(own_refs[-1][: 2 * HEADS, :])
+    queries = rounded(own_refs[-1][x if own_refs[-1].shape[0] > 1 else 0, : 2 * HEADS, :])
     scores = [jnp.sum(queries * spread(ref, 2 * HEADS), axis=1, keepdims=True) * SCALE for ref in own_refs]
     whole_top = functools.reduce(jnp.maximum, scores, top)
     factor = jnp.exp(top - whole_top)
@@ -356,19 +399,27 @@
             pieces, output = kernel_call(
                 next_kernel, [flat, shape(ROWS, width)], sums, wide, gain, w_query, w_kv, after=(other,)
             )
-        parts = exchange(pieces.reshape(GROUP, PIECE, DIM), INNER)
-        total = jnp.broadcast_to(jnp.sum(parts, axis=0)[None], (GROUP, PIECE, DIM))
-        parts = exchange(total, ("y",))
+        count = GROUP * GROUP // 2
+        block = shape(GROUP // 2, PIECE, DIM)
         if not step:
+            parts = exchange(pieces.reshape(GROUP, PIECE, DIM), INNER)
+            total = jnp.broadcast_to(jnp.sum(parts, axis=0)[None], (GROUP, PIECE, DIM))
+            parts = exchange(total, ("y",))
             other = kernel_call(swap_kernel, shape(2, ROWS // 2, seq_here, DIM), keys, values, after=(parts,))
             parts, other = lax.optimization_barrier((parts, other))
             other = lax.ppermute(other, "core", [(0, 1), (1, 0)])
-        pieces, mine = kernel_call(turn_kernel, [shape(GROUP // 2, 2 * HEADS, DIM), shape(PIECE, DIM)], parts, tables[step], after=(other,) if step else ())
+            outs = [shape(GROUP // 2, 2 * HEADS, DIM), shape(1, PIECE, DIM)]
+            pieces, mine = kernel_call(turn_kernel, outs, parts, tables[step])
+            queries = exchange(pieces, ("x",))
+            pieces = kernel_call(attend_kernel, block, queries, keys, values, other, seen, scratch=[work])
+        else:
+            parts = exchange(pieces.reshape(GROUP * GROUP, 1, SHARE * DIM), SEQ).reshape(GROUP * PIECE, DIM)
+            pieces = kernel_call(turn_shares_kernel, shape(count * SHARE, DIM), parts, tables[step], after=(other,))
+            queries = exchange(pieces.reshape(count, 1, SHARE * DIM), ("y", "x")).reshape(count * SHARE, DIM)
+            pieces, mine = kernel_call(
+                attend_kernel, [block, block], queries, keys, values, other, seen, scratch=[work]
+            )
         own.append(mine)
-        queries = exchange(pieces, ("x",))
-        pieces = kernel_call(
-            attend_kernel, shape(GROUP // 2, PIECE, DIM), queries, keys, values, other, seen, scratch=[work]
-        )
         parts = exchange(pieces, ("x",))
         kept = () if step else (other,)
         pieces = kernel_call(merge_kernel, shape(GROUP * DENSE, DIM), parts, after=kept)

time: 159 us -> 159 us (level)
    all_to_all x14 -> x13, blocking collectives: 148 us -> 148 us  [exchange(): return lax.all_to_all(pieces, axes, 0, 0, tiled=True)]
where the time goes in v5:
time: 159 us; the launch traced here: 158 us
  blocking collectives  148 us (93%)
  Pallas kernels  5.54 us (3%)
  starting transfers between devices  4.57 us (3%)
    all_to_all x13, blocking collectives, exchange(): return lax.all_to_all(pieces, axes, 0, 0, tiled=True)  148 us
    pallas_call x14, Pallas kernels, kernel_call(): pl.pallas_call(body, out_shape=out_shapes, in_specs=[pl.BlockSpec(memory_...  5.54 us
    ppermute x1, starting transfers between devices, per_device(): other = lax.ppermute(other, 'core', [(0, 1), (1, 0)])  4.57 us
  transfers between devices with their start and end apart: 1, of which 0 were waited for; matrix products, arithmetic and copies ran while one was open for 0% of the time, Pallas kernels for 0%

profile of v5, /device:TPU:1, one launch (start us, length us, event | category | flops | bytes accessed | tf_op | source)
XLA Modules:
  0.0 158.0 jit_solution(3502356384904346551)
XLA Ops:
  0.0 0.0 copy-start.1
  0.0 0.0 copy-start
  0.0 1.8 %shard_map.91 = (f32[320,128]{1,0:T(8,128)S(1)}, f32[16,256]{1,0:T(8,128)S(1)}, f32[8,256]{1,0:T(8,128)S(1)}, f32[8,512]{1,0:T(8,128)S(1)}, f32[8,128]{1,0:T(8,128)S(1)}, /*index=5*/f32[8,128]{1,0:T(8,128)S(1)}) custom-call(bf16[16,256]{1,0:T(8,128)(2,1)} %tokens_hbm.1, bf16[256]{0:T(256)(128)(2,1)} %gain_hbm.1, bf16[256,2048]{1,0:T(8,128)(2,1)} %refs_3_.1, ...), custom_call_target="tpu_custom_call" | custom-call | tf_op jit(solution)/shard_map/pallas_call | solution.py:46
  1.8 14.8 %all_to_all.65 = f32[8,40,128]{2,1,0:T(8,128)S(1)} all-to-all(f32[8,40,128]{2,1,0:T(8,128)S(1)} %bitcast.28), channel_id=1, replica_groups=mesh['heads'=8,'y'=8,'x'=4,'core'=2] {'x','core'}, dimensions={0} | all-to-all | bytes 327680 | tf_op jit(solution)/shard_map/all_to_all | solution.py:365
  16.7 11.0 %all_to_all.66.refs_2_.parts_ref = f32[8,40,128]{2,1,0:T(8,128)S(1)} all-to-all(f32[8,40,128]{2,1,0:T(8,128)S(1)} %broadcast_in_dim.2), channel_id=1, replica_groups=mesh['heads'=8,'y'=8,'x'=4,'core'=2] {'y'}, dimensions={0} | all-to-all | bytes 327680 | tf_op jit(solution)/shard_map/all_to_all | solution.py:365
  27.7 0.0 copy-done.1
  27.7 0.0 copy-done
  27.7 0.1 shard_map.92
  27.8 4.6 %collective-permute-start = (f32[2,8,256,128]{3,2,1,0:T(8,128)S(1)}, f32[2,8,256,128]{3,2,1,0:T(8,128)S(1)}, u32[]{:S(2)}, u32[]{:S(2)}) collective-permute-start(f32[2,8,256,128]{3,2,1,0:T(8,128)S(1)} %shard_map.92), channel_id=1, source_target_pairs={{0,1},{1,0},{2,3},{3,2},{4,5},{5,4},{6,7},{7,6},{8,9},{9,8},{10,11... | collective-permute-start | bytes 6291464 | tf_op jit(solution)/shard_map/ppermute | solution.py:410
  32.4 0.1 shard_map.93
  32.5 6.9 %all_to_all.67.queries_ref = f32[4,32,128]{2,1,0:T(8,128)S(1)} all-to-all(f32[4,32,128]{2,1,0:T(8,128)S(1)} %get-tuple-element.22), channel_id=1, replica_groups=mesh['heads'=8,'y'=8,'x'=4,'core'=2] {'x'}, dimensions={0} | all-to-all | bytes 131072 | tf_op jit(solution)/shard_map/all_to_all | solution.py:365
  39.4 0.0 collective-permute-done.other_ref.refs_1_.refs_2_.refs_5_
  39.4 0.6 shard_map.94
  40.0 6.9 %all_to_all.68.refs_0_ = f32[4,40,128]{2,1,0:T(8,128)S(1)} all-to-all(f32[4,40,128]{2,1,0:T(8,128)S(1)} %shard_map.94), channel_id=1, replica_groups=mesh['heads'=8,'y'=8,'x'=4,'core'=2] {'x'}, dimensions={0} | all-to-all | bytes 163840 | tf_op jit(solution)/shard_map/all_to_all | solution.py:365
  46.9 0.0 copy-start.2
  46.9 0.1 shard_map.95
  47.1 10.6 %all_to_all.69 = f32[8,1,4224]{2,1,0:T(1,128)S(1)} all-to-all(f32[8,1,4224]{2,1,0:T(1,128)S(1)} %bitcast.21), channel_id=1, replica_groups=mesh['heads'=8,'y'=8,'x'=4,'core'=2] {'y'}, dimensions={0} | all-to-all | bytes 270336 | tf_op jit(solution)/shard_map/all_to_all | solution.py:365
  57.7 0.2 shard_map.96
  57.9 0.0 copy-start.3
  57.9 0.0 copy-start.4
  57.9 11.1 %all_to_all.70 = f32[8,32,128]{2,1,0:T(8,128)S(1)} all-to-all(f32[8,32,128]{2,1,0:T(8,128)S(1)} %shard_map.96), channel_id=1, replica_groups=mesh['heads'=8,'y'=8,'x'=4,'core'=2] {'x','core'}, dimensions={0} | all-to-all | bytes 262144 | tf_op jit(solution)/shard_map/all_to_all | solution.py:365
  69.0 0.0 copy-done.2
  69.0 0.3 shard_map.97
  69.3 17.7 %all_to_all.71.refs_0_ = f32[8,16,256]{2,1,0:T(8,128)S(1)} all-to-all(f32[8,16,256]{2,1,0:T(8,128)S(1)} %shard_map.97), channel_id=1, replica_groups=mesh['heads'=8,'y'=8,'x'=4,'core'=2] {'heads'}, dimensions={0} | all-to-all | bytes 262144 | tf_op jit(solution)/shard_map/all_to_all | solution.py:365
  87.0 0.0 copy-done.3
  87.0 0.0 copy-done.4
  87.0 0.3 shard_map.98
  87.3 17.4 %all_to_all.72 = f32[64,1,640]{2,1,0:T(1,128)S(1)} all-to-all(f32[64,1,640]{2,1,0:T(1,128)S(1)} %bitcast.29), channel_id=1, replica_groups=mesh['heads'=8,'y'=8,'x'=4,'core'=2] {'y','x','core'}, dimensions={0} | all-to-all | bytes 327680 | tf_op jit(solution)/shard_map/all_to_all | solution.py:365
  104.6 0.1 shard_map.99
  104.7 12.0 %all_to_all.73 = f32[32,1,640]{2,1,0:T(1,128)S(1)} all-to-all(f32[32,1,640]{2,1,0:T(1,128)S(1)} %bitcast.26), channel_id=1, replica_groups=mesh['heads'=8,'y'=8,'x'=4,'core'=2] {'y','x'}, dimensions={0} | all-to-all | bytes 163840 | tf_op jit(solution)/shard_map/all_to_all | solution.py:365
  116.7 0.6 shard_map.100
  117.4 6.9 %all_to_all.74.parts_ref = f32[4,40,128]{2,1,0:T(8,128)S(1)} all-to-all(f32[4,40,128]{2,1,0:T(8,128)S(1)} %get-tuple-element.30), channel_id=1, replica_groups=mesh['heads'=8,'y'=8,'x'=4,'core'=2] {'x'}, dimensions={0} | all-to-all | bytes 163840 | tf_op jit(solution)/shard_map/all_to_all | solution.py:365
  124.3 0.1 shard_map.101
  124.4 10.5 %all_to_all.75 = f32[8,1,4224]{2,1,0:T(1,128)S(1)} all-to-all(f32[8,1,4224]{2,1,0:T(1,128)S(1)} %bitcast.23), channel_id=1, replica_groups=mesh['heads'=8,'y'=8,'x'=4,'core'=2] {'y'}, dimensions={0} | all-to-all | bytes 270336 | tf_op jit(solution)/shard_map/all_to_all | solution.py:365
  134.9 0.2 shard_map.102
  135.1 11.9 %all_to_all.76 = f32[8,32,128]{2,1,0:T(8,128)S(1)} all-to-all(f32[8,32,128]{2,1,0:T(8,128)S(1)} %shard_map.102), channel_id=1, replica_groups=mesh['heads'=8,'y'=8,'x'=4,'core'=2] {'x','core'}, dimensions={0} | all-to-all | bytes 262144 | tf_op jit(solution)/shard_map/all_to_all | solution.py:365
  147.0 0.3 shard_map.103
  147.3 10.1 %all_to_all.77.sums_ref = f32[8,16,256]{2,1,0:T(8,128)S(1)} all-to-all(f32[8,16,256]{2,1,0:T(8,128)S(1)} %shard_map.103), channel_id=1, replica_groups=mesh['heads'=8,'y'=8,'x'=4,'core'=2] {'heads'}, dimensions={0} | all-to-all | bytes 262144 | tf_op jit(solution)/shard_map/all_to_all | solution.py:365
  157.4 0.6 shard_map.104
  (2 shorter events, 0.0 us)
Async XLA Ops:
  0.0 27.7 %copy-start.1 = (bf16[1,16,256,128]{3,2,1,0:T(8,128)(2,1)S(1)}, bf16[1,16,256,128]{3,2,1,0:T(8,128)(2,1)}, u32[]{:S(2)}) copy-start(bf16[1,16,256,128]{3,2,1,0:T(8,128)(2,1)} %param.15) | copy-start | bytes 3145732
  0.0 27.7 %copy-start = (bf16[1,16,256,128]{3,2,1,0:T(8,128)(2,1)S(1)}, bf16[1,16,256,128]{3,2,1,0:T(8,128)(2,1)}, u32[]{:S(2)}) copy-start(bf16[1,16,256,128]{3,2,1,0:T(8,128)(2,1)} %param.14) | copy-start | bytes 3145732
  27.8 11.5 %collective-permute-start = (f32[2,8,256,128]{3,2,1,0:T(8,128)S(1)}, f32[2,8,256,128]{3,2,1,0:T(8,128)S(1)}, u32[]{:S(2)}, u32[]{:S(2)}) collective-permute-start(f32[2,8,256,128]{3,2,1,0:T(8,128)S(1)} %shard_map.92), channel_id=1, source_target_pairs={{0,1},{1,0},{2,3},{3,2},{4,5},{5,4},{6,7},{7,6},{8,9},{9,8},{10,11... | collective-permute-start | bytes 6291464 | tf_op jit(solution)/shard_map/ppermute | solution.py:410
  46.9 22.1 %copy-start.2 = (bf16[2048,256]{1,0:T(8,128)(2,1)S(1)}, bf16[2048,256]{1,0:T(8,128)(2,1)}, u32[]{:S(2)}) copy-start(bf16[2048,256]{1,0:T(8,128)(2,1)} %wout_ref.1) | copy-start | bytes 3145732
  57.9 29.1 %copy-start.3 = (bf16[256,2048]{1,0:T(8,128)(2,1)S(1)}, bf16[256,2048]{1,0:T(8,128)(2,1)}, u32[]{:S(2)}) copy-start(bf16[256,2048]{1,0:T(8,128)(2,1)} %refs_3_.1) | copy-start | bytes 3145732
  57.9 29.1 %copy-start.4 = (bf16[256,256]{1,0:T(8,128)(2,1)S(1)}, bf16[256,256]{1,0:T(8,128)(2,1)}, u32[]{:S(2)}) copy-start(bf16[256,256]{1,0:T(8,128)(2,1)} %refs_4_.1) | copy-start | bytes 393220

commit v6 on v5

--- a/solution.py
+++ b/solution.py
@@ -26,6 +26,7 @@
 BATCH = 2
 CHUNKS = 2
 DENSE = 33
+CLOSE = 34
 SHARE = 5
 QUARTER = HEADS // 4
 SCALE = 1.0 / math.sqrt(DIM)
@@ -280,11 +281,13 @@
             top = tops[b : b + OWN].reshape(OWN * HEADS, 1)
             total = totals[b : b + OWN].reshape(OWN * HEADS, 1)
             stats = joined(to_lanes(top), to_lanes(total))
-            pieces_ref[(c + b) // OWN, 2 * HEADS :, :] = jnp.broadcast_to(stats, (PIECE - 2 * HEADS, DIM))
+            end = ((c + b) // OWN + 1) * CLOSE
+            pieces_ref[end - CLOSE + 2 * HEADS : end, :] = jnp.broadcast_to(stats, (CLOSE - 2 * HEADS, DIM))
     for i in range(ROWS // 2):
         x, heads = place(i)
         own, other = (work_ref[i, :, half].astype(BF16) for half in halves)
-        pieces_ref[x, heads, :] = jnp.dot(
+        begin = x * CLOSE + heads.start
+        pieces_ref[begin : begin + HEADS, :] = jnp.dot(
             own, values_ref[core_row(i, core)], preferred_element_type=F32
         ) + jnp.dot(other, other_ref[1, i].astype(BF16), preferred_element_type=F32)
 
@@ -303,7 +306,8 @@
 
 def merge_kernel(parts_ref, pieces_ref):
     top, total, weighted = merge(*zip(*[
-        (parts_ref[s, : 2 * HEADS, :], parts_ref[s, 2 * HEADS : 2 * HEADS + 1, :]) for s in range(parts_ref.shape[0])
+        (parts_ref[s : s + 2 * HEADS, :], parts_ref[s + 2 * HEADS : s + 2 * HEADS + 1, :])
+        for s in range(0, parts_ref.shape[0], CLOSE)
     ]))
     stats = joined(top, total)
     for d in range(GROUP):
@@ -401,6 +405,7 @@
             )
         count = GROUP * GROUP // 2
         block = shape(GROUP // 2, PIECE, DIM)
+        close = shape(GROUP // 2 * CLOSE, DIM)
         if not step:
             parts = exchange(pieces.reshape(GROUP, PIECE, DIM), INNER)
             total = jnp.broadcast_to(jnp.sum(parts, axis=0)[None], (GROUP, PIECE, DIM))
@@ -411,16 +416,16 @@
             outs = [shape(GROUP // 2, 2 * HEADS, DIM), shape(1, PIECE, DIM)]
             pieces, mine = kernel_call(turn_kernel, outs, parts, tables[step])
             queries = exchange(pieces, ("x",))
-            pieces = kernel_call(attend_kernel, block, queries, keys, values, other, seen, scratch=[work])
+            pieces = kernel_call(attend_kernel, close, queries, keys, values, other, seen, scratch=[work])
         else:
             parts = exchange(pieces.reshape(GROUP * GROUP, 1, SHARE * DIM), SEQ).reshape(GROUP * PIECE, DIM)
             pieces = kernel_call(turn_shares_kernel, shape(count * SHARE, DIM), parts, tables[step], after=(other,))
             queries = exchange(pieces.reshape(count, 1, SHARE * DIM), ("y", "x")).reshape(count * SHARE, DIM)
             pieces, mine = kernel_call(
-                attend_kernel, [block, block], queries, keys, values, other, seen, scratch=[work]
+                attend_kernel, [close, block], queries, keys, values, other, seen, scratch=[work]
             )
         own.append(mine)
-        parts = exchange(pieces, ("x",))
+        parts = exchange(pieces.reshape(GROUP // 2, 1, CLOSE * DIM), ("x",)).reshape(GROUP // 2 * CLOSE, DIM)
         kept = () if step else (other,)
         pieces = kernel_call(merge_kernel, shape(GROUP * DENSE, DIM), parts, after=kept)
         parts = exchange(pieces.reshape(GROUP, 1, DENSE * DIM), ("y",)).reshape(GROUP * DENSE, DIM)

time: 159 us -> 159 us (level)
  no operation moved by 1% of the time
where the time goes in v6:
time: 159 us; the launch traced here: 158 us
  blocking collectives  148 us (93%)
  Pallas kernels  5.59 us (4%)
  starting transfers between devices  4.57 us (3%)
    all_to_all x13, blocking collectives, exchange(): return lax.all_to_all(pieces, axes, 0, 0, tiled=True)  148 us
    pallas_call x14, Pallas kernels, kernel_call(): pl.pallas_call(body, out_shape=out_shapes, in_specs=[pl.BlockSpec(memory_...  5.59 us
    ppermute x1, starting transfers between devices, per_device(): other = lax.ppermute(other, 'core', [(0, 1), (1, 0)])  4.57 us
  transfers between devices with their start and end apart: 1, of which 0 were waited for; matrix products, arithmetic and copies ran while one was open for 0% of the time, Pallas kernels for 0%

profile of v6, /device:TPU:1, one launch (start us, length us, event | category | flops | bytes accessed | tf_op | source)
XLA Modules:
  0.0 158.0 jit_solution(14421965447409096914)
XLA Ops:
  0.0 0.0 copy-start.1
  0.0 0.0 copy-start
  0.0 1.8 %shard_map.91 = (f32[320,128]{1,0:T(8,128)S(1)}, f32[16,256]{1,0:T(8,128)S(1)}, f32[8,256]{1,0:T(8,128)S(1)}, f32[8,512]{1,0:T(8,128)S(1)}, f32[8,128]{1,0:T(8,128)S(1)}, /*index=5*/f32[8,128]{1,0:T(8,128)S(1)}) custom-call(bf16[16,256]{1,0:T(8,128)(2,1)} %tokens_hbm.1, bf16[256]{0:T(256)(128)(2,1)} %gain_hbm.1, bf16[256,2048]{1,0:T(8,128)(2,1)} %refs_3_.1, ...), custom_call_target="tpu_custom_call" | custom-call | tf_op jit(solution)/shard_map/pallas_call | solution.py:47
  1.8 14.8 %all_to_all.65 = f32[8,40,128]{2,1,0:T(8,128)S(1)} all-to-all(f32[8,40,128]{2,1,0:T(8,128)S(1)} %bitcast.35), channel_id=1, replica_groups=mesh['heads'=8,'y'=8,'x'=4,'core'=2] {'x','core'}, dimensions={0} | all-to-all | bytes 327680 | tf_op jit(solution)/shard_map/all_to_all | solution.py:369
  16.7 11.0 %all_to_all.66.refs_2_.parts_ref = f32[8,40,128]{2,1,0:T(8,128)S(1)} all-to-all(f32[8,40,128]{2,1,0:T(8,128)S(1)} %broadcast_in_dim.2), channel_id=1, replica_groups=mesh['heads'=8,'y'=8,'x'=4,'core'=2] {'y'}, dimensions={0} | all-to-all | bytes 327680 | tf_op jit(solution)/shard_map/all_to_all | solution.py:369
  27.7 0.0 copy-done.1
  27.7 0.0 copy-done
  27.7 0.1 shard_map.92
  27.8 4.6 %collective-permute-start = (f32[2,8,256,128]{3,2,1,0:T(8,128)S(1)}, f32[2,8,256,128]{3,2,1,0:T(8,128)S(1)}, u32[]{:S(2)}, u32[]{:S(2)}) collective-permute-start(f32[2,8,256,128]{3,2,1,0:T(8,128)S(1)} %shard_map.92), channel_id=1, source_target_pairs={{0,1},{1,0},{2,3},{3,2},{4,5},{5,4},{6,7},{7,6},{8,9},{9,8},{10,11... | collective-permute-start | bytes 6291464 | tf_op jit(solution)/shard_map/ppermute | solution.py:415
  32.4 0.1 shard_map.93
  32.5 6.9 %all_to_all.67.queries_ref = f32[4,32,128]{2,1,0:T(8,128)S(1)} all-to-all(f32[4,32,128]{2,1,0:T(8,128)S(1)} %get-tuple-element.22), channel_id=1, replica_groups=mesh['heads'=8,'y'=8,'x'=4,'core'=2] {'x'}, dimensions={0} | all-to-all | bytes 131072 | tf_op jit(solution)/shard_map/all_to_all | solution.py:369
  39.4 0.0 collective-permute-done.other_ref.refs_1_.refs_2_.refs_5_
  39.4 0.7 shard_map.94
  40.0 6.9 %all_to_all.68 = f32[4,1,4352]{2,1,0:T(1,128)S(1)} all-to-all(f32[4,1,4352]{2,1,0:T(1,128)S(1)} %bitcast.32), channel_id=1, replica_groups=mesh['heads'=8,'y'=8,'x'=4,'core'=2] {'x'}, dimensions={0} | all-to-all | bytes 139264 | tf_op jit(solution)/shard_map/all_to_all | solution.py:369
  46.9 0.0 copy-start.2
  46.9 0.1 shard_map.95
  47.0 10.6 %all_to_all.69 = f32[8,1,4224]{2,1,0:T(1,128)S(1)} all-to-all(f32[8,1,4224]{2,1,0:T(1,128)S(1)} %bitcast.25), channel_id=1, replica_groups=mesh['heads'=8,'y'=8,'x'=4,'core'=2] {'y'}, dimensions={0} | all-to-all | bytes 270336 | tf_op jit(solution)/shard_map/all_to_all | solution.py:369
  57.6 0.2 shard_map.96
  57.8 0.0 copy-start.3
  57.9 0.0 copy-start.4
  57.9 11.1 %all_to_all.70 = f32[8,32,128]{2,1,0:T(8,128)S(1)} all-to-all(f32[8,32,128]{2,1,0:T(8,128)S(1)} %shard_map.96), channel_id=1, replica_groups=mesh['heads'=8,'y'=8,'x'=4,'core'=2] {'x','core'}, dimensions={0} | all-to-all | bytes 262144 | tf_op jit(solution)/shard_map/all_to_all | solution.py:369
  69.0 0.0 copy-done.2
  69.0 0.3 shard_map.97
  69.3 17.7 %all_to_all.71.refs_0_ = f32[8,16,256]{2,1,0:T(8,128)S(1)} all-to-all(f32[8,16,256]{2,1,0:T(8,128)S(1)} %shard_map.97), channel_id=1, replica_groups=mesh['heads'=8,'y'=8,'x'=4,'core'=2] {'heads'}, dimensions={0} | all-to-all | bytes 262144 | tf_op jit(solution)/shard_map/all_to_all | solution.py:369
  87.0 0.0 copy-done.3
  87.0 0.0 copy-done.4
  87.0 0.3 shard_map.98
  87.2 17.4 %all_to_all.72 = f32[64,1,640]{2,1,0:T(1,128)S(1)} all-to-all(f32[64,1,640]{2,1,0:T(1,128)S(1)} %bitcast.36), channel_id=1, replica_groups=mesh['heads'=8,'y'=8,'x'=4,'core'=2] {'y','x','core'}, dimensions={0} | all-to-all | bytes 327680 | tf_op jit(solution)/shard_map/all_to_all | solution.py:369
  104.6 0.1 shard_map.99
  104.7 12.0 %all_to_all.73 = f32[32,1,640]{2,1,0:T(1,128)S(1)} all-to-all(f32[32,1,640]{2,1,0:T(1,128)S(1)} %bitcast.30), channel_id=1, replica_groups=mesh['heads'=8,'y'=8,'x'=4,'core'=2] {'y','x'}, dimensions={0} | all-to-all | bytes 163840 | tf_op jit(solution)/shard_map/all_to_all | solution.py:369
  116.7 0.7 shard_map.100
  117.3 6.9 %all_to_all.74 = f32[4,1,4352]{2,1,0:T(1,128)S(1)} all-to-all(f32[4,1,4352]{2,1,0:T(1,128)S(1)} %bitcast.37), channel_id=1, replica_groups=mesh['heads'=8,'y'=8,'x'=4,'core'=2] {'x'}, dimensions={0} | all-to-all | bytes 139264 | tf_op jit(solution)/shard_map/all_to_all | solution.py:369
  124.2 0.1 shard_map.101
  124.3 10.5 %all_to_all.75 = f32[8,1,4224]{2,1,0:T(1,128)S(1)} all-to-all(f32[8,1,4224]{2,1,0:T(1,128)S(1)} %bitcast.26), channel_id=1, replica_groups=mesh['heads'=8,'y'=8,'x'=4,'core'=2] {'y'}, dimensions={0} | all-to-all | bytes 270336 | tf_op jit(solution)/shard_map/all_to_all | solution.py:369
  134.8 0.2 shard_map.102
  135.0 11.9 %all_to_all.76 = f32[8,32,128]{2,1,0:T(8,128)S(1)} all-to-all(f32[8,32,128]{2,1,0:T(8,128)S(1)} %shard_map.102), channel_id=1, replica_groups=mesh['heads'=8,'y'=8,'x'=4,'core'=2] {'x','core'}, dimensions={0} | all-to-all | bytes 262144 | tf_op jit(solution)/shard_map/all_to_all | solution.py:369
  146.9 0.3 shard_map.103
  147.2 10.1 %all_to_all.77.sums_ref = f32[8,16,256]{2,1,0:T(8,128)S(1)} all-to-all(f32[8,16,256]{2,1,0:T(8,128)S(1)} %shard_map.103), channel_id=1, replica_groups=mesh['heads'=8,'y'=8,'x'=4,'core'=2] {'heads'}, dimensions={0} | all-to-all | bytes 262144 | tf_op jit(solution)/shard_map/all_to_all | solution.py:369
  157.3 0.6 shard_map.104
  (2 shorter events, 0.0 us)
Async XLA Ops:
  0.0 27.7 %copy-start.1 = (bf16[1,16,256,128]{3,2,1,0:T(8,128)(2,1)S(1)}, bf16[1,16,256,128]{3,2,1,0:T(8,128)(2,1)}, u32[]{:S(2)}) copy-start(bf16[1,16,256,128]{3,2,1,0:T(8,128)(2,1)} %param.15) | copy-start | bytes 3145732
  0.0 27.7 %copy-start = (bf16[1,16,256,128]{3,2,1,0:T(8,128)(2,1)S(1)}, bf16[1,16,256,128]{3,2,1,0:T(8,128)(2,1)}, u32[]{:S(2)}) copy-start(bf16[1,16,256,128]{3,2,1,0:T(8,128)(2,1)} %param.14) | copy-start | bytes 3145732
  27.8 11.5 %collective-permute-start = (f32[2,8,256,128]{3,2,1,0:T(8,128)S(1)}, f32[2,8,256,128]{3,2,1,0:T(8,128)S(1)}, u32[]{:S(2)}, u32[]{:S(2)}) collective-permute-start(f32[2,8,256,128]{3,2,1,0:T(8,128)S(1)} %shard_map.92), channel_id=1, source_target_pairs={{0,1},{1,0},{2,3},{3,2},{4,5},{5,4},{6,7},{7,6},{8,9},{9,8},{10,11... | collective-permute-start | bytes 6291464 | tf_op jit(solution)/shard_map/ppermute | solution.py:415
  46.9 22.1 %copy-start.2 = (bf16[2048,256]{1,0:T(8,128)(2,1)S(1)}, bf16[2048,256]{1,0:T(8,128)(2,1)}, u32[]{:S(2)}) copy-start(bf16[2048,256]{1,0:T(8,128)(2,1)} %wout_ref.1) | copy-start | bytes 3145732
  57.8 29.1 %copy-start.3 = (bf16[256,2048]{1,0:T(8,128)(2,1)S(1)}, bf16[256,2048]{1,0:T(8,128)(2,1)}, u32[]{:S(2)}) copy-start(bf16[256,2048]{1,0:T(8,128)(2,1)} %refs_3_.1) | copy-start | bytes 3145732
  57.9 29.1 %copy-start.4 = (bf16[256,256]{1,0:T(8,128)(2,1)S(1)}, bf16[256,256]{1,0:T(8,128)(2,1)}, u32[]{:S(2)}) copy-start(bf16[256,256]{1,0:T(8,128)(2,1)} %refs_4_.1) | copy-start | bytes 393220
